TPU v7x, 256 devices: a whole 4x4x8 slice. The times are simulated.
256 devices in a mesh: grp: 4 (over y_hi, core), tile: 64 (over y_lo, x, z).
Axes of the slice: x: 4, y: 4 (y_hi: 2, y_lo: 2; y = y_hi * 2 + y_lo), z: 8, core: 2. Of those that a mesh axis runs over, the one named last changes fastest.
Arguments:
- query_tokens: bfloat16 [24576, 3072], P('tile', 'grp'), may hold values from -5 to 5
- key_tokens: bfloat16 [24576, 3072], P('tile', 'grp'), may hold values from -5 to 5
- value_tokens: bfloat16 [24576, 3072], P('tile', 'grp'), may hold values from -6 to 6
- w_out: bfloat16 [3072, 1536], P('grp'), may hold values from -1.75 to 1.75
- cotangent: bfloat16 [24576, 1536], P('tile', 'grp'), may hold values from -1.5 to 1.5
- neighbours: int32 [64, 5], P('tile'), may hold values from -1 to 63, as said below
- tile_tokens: int32 [64], replicated, may hold values from 1 to 384, as said below
Outputs:
- block_out: bfloat16 [24576, 1536], P('tile', 'grp')
- query_grad: bfloat16 [24576, 3072], P('tile', 'grp')
- key_grad: bfloat16 [24576, 3072], P('tile', 'grp')
- value_grad: bfloat16 [24576, 3072], P('tile', 'grp')
- weight_grad: bfloat16 [3072, 1536], P('grp')
Inputs may be any that keep to these rules, and one draw needn't show every extreme that they name: `neighbours`: row r lists distinct tiles: first r itself, then tiles at most one tile away from r in time, height and width; unused slots come last and hold -1; some rows use all 5 slots. `tile_tokens`: the live tokens of a tile are its first ones; every tile outside the last time tile and the last height tile holds all 384.
All inputs are finite; a program needn't handle non-finite values.
Results may differ from a plain program's by a relative error of at most 0.0074.
Values may be sent and summed in bfloat16 or wider, within the bound.
A program may use at most 192 MiB of HBM per device.

v0:
```python
import math

import jax
import jax.numpy as jnp
from jax import lax
from jax.sharding import PartitionSpec as P

HEAD_DIM = 128
TILE = 384
NB = 5
NH = 4


def from_behind(value, axis, steps):
    count = lax.axis_size(axis)
    initial, last = (max(0, -steps), min(count, count - steps))
    return lax.ppermute(value, axis, [(source, source + steps) for source in range(initial, last)])


def softmax_rows(scores, live_mask):
    masked = jnp.where(live_mask[None, :], scores, jnp.float32(-1e30))
    row_max = jnp.max(masked, axis=1, keepdims=True)
    exponent = jnp.exp(masked - row_max)
    return exponent / jnp.sum(exponent, axis=1, keepdims=True)


def head_pass(query_rows, near_keys, near_values, grad_rows, live_mask, factor):
    scores = (
        lax.dot_general(
            query_rows, near_keys, (((1,), (1,)), ((), ())), preferred_element_type=jnp.float32
        )
        * factor
    )
    probability = softmax_rows(scores, live_mask)
    weights = probability.astype(jnp.bfloat16)
    attended = jnp.dot(weights, near_values, preferred_element_type=jnp.float32).astype(
        jnp.bfloat16
    )
    grad_prob = lax.dot_general(
        grad_rows, near_values, (((1,), (1,)), ((), ())), preferred_element_type=jnp.float32
    )
    row_delta = jnp.sum(probability * grad_prob, axis=1, keepdims=True)
    dscore = (probability * (grad_prob - row_delta) * factor).astype(jnp.bfloat16)
    grad_query = jnp.dot(dscore, near_keys, preferred_element_type=jnp.float32)
    grad_keys = lax.dot_general(
        dscore, query_rows, (((0,), (0,)), ((), ())), preferred_element_type=jnp.float32
    )
    grad_values = lax.dot_general(
        weights, grad_rows, (((0,), (0,)), ((), ())), preferred_element_type=jnp.float32
    )
    return (attended, grad_query, grad_keys, grad_values)


def columns(matrix, first_col):
    return lax.dynamic_slice_in_dim(matrix, first_col, HEAD_DIM, 1)


def body(query_tokens, key_tokens, value_tokens, w_out, cotangent, neighbours, tile_tokens):
    rows_here = query_tokens.shape[0]
    width_here = query_tokens.shape[1]
    tiles_here = rows_here // TILE
    heads_here = width_here // HEAD_DIM
    factor = 1.0 / math.sqrt(HEAD_DIM)
    device_pos = lax.axis_index("tile")
    time_here = device_pos // NH
    height_here = device_pos % NH
    offsets = [
        (row_step - 1) * NH + (col_step - 1) for row_step in range(3) for col_step in range(3)
    ]
    paired = jnp.stack([key_tokens, value_tokens])
    blocks = []
    for offset in offsets:
        if offset == 0:
            blocks.append(paired)
        else:
            blocks.append(from_behind(paired, "tile", -offset))
    halo_blocks = jnp.stack(blocks)
    key_blocks = halo_blocks[:, 0]
    value_blocks = halo_blocks[:, 1]
    cot_full = lax.all_gather(cotangent, "grp", axis=1, tiled=True)
    grad_attn = lax.dot_general(
        cot_full, w_out, (((1,), (1,)), ((), ())), preferred_element_type=jnp.float32
    ).astype(jnp.bfloat16)
    query_tiles = query_tokens.reshape(tiles_here, TILE, width_here)
    grad_tiles = grad_attn.reshape(tiles_here, TILE, width_here)
    positions = jnp.arange(TILE, dtype=jnp.int32)
    all_tiles = jnp.arange(tile_tokens.shape[0], dtype=jnp.int32)

    def tile_step(buffers, width_pos):
        key_buffer, value_buffer = buffers
        list_ids = lax.dynamic_index_in_dim(neighbours, width_pos, 0, keepdims=False)
        safe_ids = jnp.maximum(list_ids, 0)
        near_time = safe_ids // (NH * tiles_here)
        near_height = safe_ids // tiles_here % NH
        near_width = safe_ids % tiles_here
        slot_index = (
            (near_time - time_here + 1) * 3 + (near_height - height_here + 1)
        ) * tiles_here + near_width
        slot_index = jnp.where(list_ids >= 0, slot_index, 4 * tiles_here)
        counts = jnp.sum(
            jnp.where(safe_ids[:, None] == all_tiles[None, :], tile_tokens[None, :], 0), axis=1
        )
        live_mask = ((list_ids >= 0)[:, None] & (positions[None, :] < counts[:, None])).reshape(-1)
        near_keys = key_blocks[slot_index].reshape(-1, width_here)
        near_values = value_blocks[slot_index].reshape(-1, width_here)
        query_tile = lax.dynamic_index_in_dim(query_tiles, width_pos, 0, keepdims=False)
        grad_tile = lax.dynamic_index_in_dim(grad_tiles, width_pos, 0, keepdims=False)

        def head_step(head_pos, results):
            out_rows, dq_rows, dk_rows, dv_rows = results
            first_col = head_pos * HEAD_DIM
            attended, grad_query, grad_keys, grad_values = head_pass(
                columns(query_tile, first_col),
                columns(near_keys, first_col),
                columns(near_values, first_col),
                columns(grad_tile, first_col),
                live_mask,
                factor,
            )
            out_rows = lax.dynamic_update_slice_in_dim(out_rows, attended, first_col, 1)
            dq_rows = lax.dynamic_update_slice_in_dim(
                dq_rows, grad_query.astype(jnp.bfloat16), first_col, 1
            )
            dk_rows = lax.dynamic_update_slice_in_dim(dk_rows, grad_keys, first_col, 1)
            dv_rows = lax.dynamic_update_slice_in_dim(dv_rows, grad_values, first_col, 1)
            return (out_rows, dq_rows, dk_rows, dv_rows)

        initial = (
            jnp.zeros((TILE, width_here), jnp.bfloat16),
            jnp.zeros((TILE, width_here), jnp.bfloat16),
            jnp.zeros((NB * TILE, width_here), jnp.float32),
            jnp.zeros((NB * TILE, width_here), jnp.float32),
        )
        out_rows, dq_rows, dk_rows, dv_rows = lax.fori_loop(0, heads_here, head_step, initial)
        key_buffer = key_buffer.at[slot_index].add(dk_rows.reshape(-1, TILE, width_here))
        value_buffer = value_buffer.at[slot_index].add(dv_rows.reshape(-1, TILE, width_here))
        return ((key_buffer, value_buffer), (out_rows, dq_rows))

    zero_buffer = jnp.zeros((9 * tiles_here, TILE, width_here), jnp.float32)
    (key_buffer, value_buffer), (out_tiles, dq_tiles) = lax.scan(
        tile_step, (zero_buffer, zero_buffer), jnp.arange(tiles_here, dtype=jnp.int32)
    )
    attended = out_tiles.reshape(rows_here, width_here)
    key_total = key_buffer[4]
    value_total = value_buffer[4]
    sent_slots = jnp.stack([key_buffer, value_buffer], axis=1).astype(jnp.bfloat16)
    for slot_pos in range(9):
        offset = offsets[slot_pos]
        if offset != 0:
            returned = from_behind(sent_slots[slot_pos], "tile", offset)
            key_total = key_total + returned[0].astype(jnp.float32)
            value_total = value_total + returned[1].astype(jnp.float32)
    partial_out = jnp.dot(attended, w_out, preferred_element_type=jnp.float32)
    block_out = lax.psum_scatter(partial_out, "grp", scatter_dimension=1, tiled=True).astype(
        jnp.bfloat16
    )
    weight_part = lax.dot_general(
        attended, cot_full, (((0,), (0,)), ((), ())), preferred_element_type=jnp.float32
    )
    weight_grad = lax.psum(weight_part, "tile").astype(jnp.bfloat16)
    query_grad = dq_tiles.reshape(rows_here, width_here)
    return (
        block_out,
        query_grad,
        key_total.astype(jnp.bfloat16),
        value_total.astype(jnp.bfloat16),
        weight_grad,
    )


def solution(mesh):
    placed = (
        P("tile", "grp"),
        P("tile", "grp"),
        P("tile", "grp"),
        P("grp", None),
        P("tile", "grp"),
        P("tile", None),
        P(),
    )
    return jax.shard_map(
        body,
        mesh=mesh,
        in_specs=placed,
        out_specs=(
            P("tile", "grp"),
            P("tile", "grp"),
            P("tile", "grp"),
            P("tile", "grp"),
            P("grp", None),
        ),
        check_vma=False,
    )
```

profile of v0, /device:TPU:24, one launch (start us, length us, event | category | flops | bytes accessed | tf_op | source)
XLA Modules:
  0.0 1153.2 jit_solution(3002877266105856304)
XLA Ops:
  8.8 8.7 collective-permute-start
  19.9 6.5 collective-permute-start.2
  30.6 5.9 collective-permute-start.4
  37.5 107.0 %collective-permute-done = bf16[2,384,768]{2,1,0:T(8,128)(2,1)} collective-permute-done((bf16[2,384,768]{2,1,0:T(8,128)(2,1)S(1)}, bf16[2,384,768]{2,1,0:T(8,128)(2,1)}, u32[]{:S(2)}, u32[]{:S(2)}) %collective-permute-start) | collective-permute-done | bytes 1179680 | tf_op jit(solution)/shard_map/ppermute | solution.py:17
  144.6 9.8 collective-permute-start.5
  165.5 44.9 %collective-permute-done.3 = bf16[2,384,768]{2,1,0:T(8,128)(2,1)} collective-permute-done((bf16[2,384,768]{2,1,0:T(8,128)(2,1)S(1)}, bf16[2,384,768]{2,1,0:T(8,128)(2,1)}, u32[]{:S(2)}, u32[]{:S(2)}) %collective-permute-start.3) | collective-permute-done | bytes 1179680 | tf_op jit(solution)/shard_map/ppermute | solution.py:17
  216.3 47.9 %collective-permute-done.5 = bf16[2,384,768]{2,1,0:T(8,128)(2,1)S(1)} collective-permute-done((bf16[2,384,768]{2,1,0:T(8,128)(2,1)S(1)}, bf16[2,384,768]{2,1,0:T(8,128)(2,1)S(1)}, u32[]{:S(2)}, u32[]{:S(2)}) %collective-permute-start.5) | collective-permute-done | bytes 1179680 | tf_op jit(solution)/shard_map/ppermute | solution.py:17
  266.5 41.2 %collective-permute-done.7 = bf16[2,384,768]{2,1,0:T(8,128)(2,1)S(1)} collective-permute-done((bf16[2,384,768]{2,1,0:T(8,128)(2,1)S(1)}, bf16[2,384,768]{2,1,0:T(8,128)(2,1)S(1)}, u32[]{:S(2)}, u32[]{:S(2)}) %collective-permute-start.7) | collective-permute-done | bytes 1179680 | tf_op jit(solution)/shard_map/ppermute | solution.py:17
  308.8 8.9 slice_bitcast_fusion
  317.7 5.1 gather_fusion
  322.8 5.0 gather_fusion.1
  336.9 83.1 %while.33 = (s32[]{:T(128)}, bf16[384,768]{1,0:T(8,128)(2,1)S(1)}, bf16[384,768]{1,0:T(8,128)(2,1)S(1)}, f32[1920,768]{1,0:T(8,128)}, f32[1920,768]{1,0:T(8,128)...) while((s32[]{:T(128)}, bf16[384,768]{1,0:T(8,128)(2,1)S(1)}, ...), condition=%wide.region_5.6_spmd.clone, body=%wide.region_1.5_spmd.clone.sunk | while | flops 1148045952 | bytes 32573652 | solution.py:134
  424.8 13.3 %scatter_fusion = f32[9,384,768]{2,1,0:T(8,128)} fusion(f32[9,384,768]{2,1,0:T(8,128)} %broadcast_in_dim.82.clone.1, s32[5]{0:T(128)S(1)} %copy-done.7, f32[5,384,768]{2,1,0:T(8,128)} %bitcast.95), kind=kCustom, calls=%fused_computation.2 | custom fusion | flops 1474560 | bytes 17694740 | tf_op jit(solution)/shard_map/while/body/eval_jaxpr/scatter-add | solution.py:135
  438.1 5.0 broadcast_in_dim.82.clone
  443.1 13.4 %scatter_fusion.1 = f32[9,384,768]{2,1,0:T(8,128)} fusion(f32[9,384,768]{2,1,0:T(8,128)} %broadcast_in_dim.82.clone, s32[5]{0:T(128)S(1)} %copy-done.7, f32[5,384,768]{2,1,0:T(8,128)} %bitcast.96), kind=kCustom, calls=%fused_computation.3 | custom fusion | flops 1474560 | bytes 17694740 | tf_op jit(solution)/shard_map/while/body/eval_jaxpr/scatter-add | solution.py:136
  456.5 7.7 convert_bitcast_fusion
  468.3 29.6 %collective-permute-start.10 = (bf16[2,384,768]{2,1,0:T(8,128)(2,1)}, bf16[2,384,768]{2,1,0:T(8,128)(2,1)}, u32[]{:S(2)}, u32[]{:S(2)}) collective-permute-start(bf16[2,384,768]{2,1,0:T(8,128)(2,1)} %get-tuple-element.295), channel_id=1, source_target_pairs={{3,0},{4,1},{5,2},{6,3},{7,4},{8,5},{9,6},{10,7},{11,8},{12,9},{13... | collective-permute-start | bytes 3538952 | tf_op jit(solution)/shard_map/ppermute | solution.py:17
  505.8 5.8 collective-permute-start.14
  517.7 47.2 %collective-permute-done.10 = bf16[2,384,768]{2,1,0:T(8,128)(2,1)} collective-permute-done((bf16[2,384,768]{2,1,0:T(8,128)(2,1)}, bf16[2,384,768]{2,1,0:T(8,128)(2,1)}, u32[]{:S(2)}, u32[]{:S(2)}) %collective-permute-start.10) | collective-permute-done | bytes 1179680 | tf_op jit(solution)/shard_map/ppermute | solution.py:17
  564.8 6.9 collective-permute-start.15
  571.7 85.5 %collective-permute-done.11 = bf16[2,384,768]{2,1,0:T(8,128)(2,1)} collective-permute-done((bf16[2,384,768]{2,1,0:T(8,128)(2,1)}, bf16[2,384,768]{2,1,0:T(8,128)(2,1)}, u32[]{:S(2)}, u32[]{:S(2)}) %collective-permute-start.11) | collective-permute-done | bytes 1179680 | tf_op jit(solution)/shard_map/ppermute | solution.py:17
  659.1 6.5 collective-permute-start.9
  665.6 472.8 %all-reduce.1 = bf16[768,1536]{1,0:T(8,128)(2,1)} all-reduce(f32[768,1536]{1,0:T(8,128)} %fusion.53), channel_id=1, replica_groups=mesh['grp'=4,'tile'=64] {'tile'}, use_global_device_ids=true, to_apply=%region_9.10 | all-reduce | flops 1179648 | bytes 7077888 | tf_op jit(solution)/shard_map/psum | solution.py:160
  1138.5 6.0 fusion.45
  (129 shorter events, 147.8 us)
Async XLA Ops:
  7.2 320.6 %copy-start = (bf16[768,1536]{1,0:T(8,128)(2,1)S(1)}, bf16[768,1536]{1,0:T(8,128)(2,1)}, u32[]{:S(2)}) copy-start(bf16[768,1536]{1,0:T(8,128)(2,1)} %param.12) | copy-start | bytes 7077892
  7.2 320.6 %all-gather.2.cloned.1.call-start = ((), (), s32[]{:S(2)}) async-start(), calls=%async_computation.1 | async-start | bytes 1474560 | tf_op jit(solution)/shard_map/all_gather | solution.py:80
  8.8 135.8 %collective-permute-start = (bf16[2,384,768]{2,1,0:T(8,128)(2,1)S(1)}, bf16[2,384,768]{2,1,0:T(8,128)(2,1)}, u32[]{:S(2)}, u32[]{:S(2)}) collective-permute-start(bf16[2,384,768]{2,1,0:T(8,128)(2,1)S(1)} %pad_maximum_fusion.1), channel_id=1, source_target_pairs={{0,5},{1,6},{2,7},{3,8},{4,9},{5,10},{6,11},{7,12},{8,13},{9,14},{... | collective-permute-start | bytes 3538952 | tf_op jit(solution)/shard_map/ppermute | solution.py:17
  17.4 139.3 %collective-permute-start.1 = (bf16[2,384,768]{2,1,0:T(8,128)(2,1)S(1)}, bf16[2,384,768]{2,1,0:T(8,128)(2,1)}, u32[]{:S(2)}, u32[]{:S(2)}) collective-permute-start(bf16[2,384,768]{2,1,0:T(8,128)(2,1)S(1)} %pad_maximum_fusion.1), channel_id=1, source_target_pairs={{0,4},{1,5},{2,6},{3,7},{4,8},{5,9},{6,10},{7,11},{8,12},{9,13},{1... | collective-permute-start | bytes 3538952 | tf_op jit(solution)/shard_map/ppermute | solution.py:17
  19.9 141.1 %collective-permute-start.2 = (bf16[2,384,768]{2,1,0:T(8,128)(2,1)S(1)}, bf16[2,384,768]{2,1,0:T(8,128)(2,1)}, u32[]{:S(2)}, u32[]{:S(2)}) collective-permute-start(bf16[2,384,768]{2,1,0:T(8,128)(2,1)S(1)} %pad_maximum_fusion.1), channel_id=1, source_target_pairs={{0,3},{1,4},{2,5},{3,6},{4,7},{5,8},{6,9},{7,10},{8,11},{9,12},{10... | collective-permute-start | bytes 3538952 | tf_op jit(solution)/shard_map/ppermute | solution.py:17
  26.4 183.9 %collective-permute-start.3 = (bf16[2,384,768]{2,1,0:T(8,128)(2,1)S(1)}, bf16[2,384,768]{2,1,0:T(8,128)(2,1)}, u32[]{:S(2)}, u32[]{:S(2)}) collective-permute-start(bf16[2,384,768]{2,1,0:T(8,128)(2,1)S(1)} %pad_maximum_fusion.1), channel_id=1, source_target_pairs={{0,1},{1,2},{2,3},{3,4},{4,5},{5,6},{6,7},{7,8},{8,9},{9,10},{10,1... | collective-permute-start | bytes 3538952 | tf_op jit(solution)/shard_map/ppermute | solution.py:17
  30.6 183.3 %collective-permute-start.4 = (bf16[2,384,768]{2,1,0:T(8,128)(2,1)S(1)}, bf16[2,384,768]{2,1,0:T(8,128)(2,1)}, u32[]{:S(2)}, u32[]{:S(2)}) collective-permute-start(bf16[2,384,768]{2,1,0:T(8,128)(2,1)S(1)} %pad_maximum_fusion.1), channel_id=1, source_target_pairs={{1,0},{2,1},{3,2},{4,3},{5,4},{6,5},{7,6},{8,7},{9,8},{10,9},{11,1... | collective-permute-start | bytes 3538952 | tf_op jit(solution)/shard_map/ppermute | solution.py:17
  36.6 1108.0 %reduce-scatter.2.cloned.1.call-start = ((), (), s32[]{:S(2)}) async-start(), calls=%async_computation.2 | async-start | bytes 2949120 | tf_op jit(solution)/shard_map/reduce_scatter | solution.py:154
  36.8 124.2 %copy-start.6 = (s32[5]{0:T(128)}, s32[5]{0:T(128)S(1)}, u32[]{:S(2)}) copy-start(s32[5]{0:T(128)S(1)} %fusion.50) | copy-start | bytes 64
  144.6 119.6 %collective-permute-start.5 = (bf16[2,384,768]{2,1,0:T(8,128)(2,1)S(1)}, bf16[2,384,768]{2,1,0:T(8,128)(2,1)S(1)}, u32[]{:S(2)}, u32[]{:S(2)}) collective-permute-start(bf16[2,384,768]{2,1,0:T(8,128)(2,1)S(1)} %pad_maximum_fusion.1), channel_id=1, source_target_pairs={{3,0},{4,1},{5,2},{6,3},{7,4},{8,5},{9,6},{10,7},{11,8},{12,9},{13... | collective-permute-start | bytes 3538952 | tf_op jit(solution)/shard_map/ppermute | solution.py:17
  156.7 108.6 %collective-permute-start.6 = (bf16[2,384,768]{2,1,0:T(8,128)(2,1)S(1)}, bf16[2,384,768]{2,1,0:T(8,128)(2,1)S(1)}, u32[]{:S(2)}, u32[]{:S(2)}) collective-permute-start(bf16[2,384,768]{2,1,0:T(8,128)(2,1)S(1)} %pad_maximum_fusion.1), channel_id=1, source_target_pairs={{4,0},{5,1},{6,2},{7,3},{8,4},{9,5},{10,6},{11,7},{12,8},{13,9},{1... | collective-permute-start | bytes 3538952 | tf_op jit(solution)/shard_map/ppermute | solution.py:17
  161.0 51.7 %copy-start.1 = (bf16[384,768]{1,0:T(8,128)(2,1)S(1)}, bf16[384,768]{1,0:T(8,128)(2,1)}, u32[]{:S(2)}) copy-start(bf16[384,768]{1,0:T(8,128)(2,1)} %param.11) | copy-start | bytes 1769476
  161.0 51.7 %copy-start.2 = (bf16[384,768]{1,0:T(8,128)(2,1)S(1)}, bf16[384,768]{1,0:T(8,128)(2,1)}, u32[]{:S(2)}) copy-start(bf16[384,768]{1,0:T(8,128)(2,1)} %param.10) | copy-start | bytes 1769476
  161.0 146.6 %collective-permute-start.7 = (bf16[2,384,768]{2,1,0:T(8,128)(2,1)S(1)}, bf16[2,384,768]{2,1,0:T(8,128)(2,1)S(1)}, u32[]{:S(2)}, u32[]{:S(2)}) collective-permute-start(bf16[2,384,768]{2,1,0:T(8,128)(2,1)S(1)} %pad_maximum_fusion.1), channel_id=1, source_target_pairs={{5,0},{6,1},{7,2},{8,3},{9,4},{10,5},{11,6},{12,7},{13,8},{14,9},{... | collective-permute-start | bytes 3538952 | tf_op jit(solution)/shard_map/ppermute | solution.py:17
  464.2 47.3 %copy-start.4 = (bf16[384,1536]{1,0:T(8,128)(2,1)S(1)}, bf16[384,1536]{1,0:T(8,128)(2,1)}, u32[]{:S(2)}) copy-start(bf16[384,1536]{1,0:T(8,128)(2,1)} %all-gather.2.cloned.1.call-done) | copy-start | bytes 3538948
  468.3 96.5 %collective-permute-start.10 = (bf16[2,384,768]{2,1,0:T(8,128)(2,1)}, bf16[2,384,768]{2,1,0:T(8,128)(2,1)}, u32[]{:S(2)}, u32[]{:S(2)}) collective-permute-start(bf16[2,384,768]{2,1,0:T(8,128)(2,1)} %get-tuple-element.295), channel_id=1, source_target_pairs={{3,0},{4,1},{5,2},{6,3},{7,4},{8,5},{9,6},{10,7},{11,8},{12,9},{13... | collective-permute-start | bytes 3538952 | tf_op jit(solution)/shard_map/ppermute | solution.py:17
  498.0 159.2 %collective-permute-start.11 = (bf16[2,384,768]{2,1,0:T(8,128)(2,1)}, bf16[2,384,768]{2,1,0:T(8,128)(2,1)}, u32[]{:S(2)}, u32[]{:S(2)}) collective-permute-start(bf16[2,384,768]{2,1,0:T(8,128)(2,1)} %get-tuple-element.294), channel_id=1, source_target_pairs={{1,0},{2,1},{3,2},{4,3},{5,4},{6,5},{7,6},{8,7},{9,8},{10,9},{11,1... | collective-permute-start | bytes 3538952 | tf_op jit(solution)/shard_map/ppermute | solution.py:17
  499.9 159.2 %collective-permute-start.12 = (bf16[2,384,768]{2,1,0:T(8,128)(2,1)}, bf16[2,384,768]{2,1,0:T(8,128)(2,1)}, u32[]{:S(2)}, u32[]{:S(2)}) collective-permute-start(bf16[2,384,768]{2,1,0:T(8,128)(2,1)} %get-tuple-element.293), channel_id=1, source_target_pairs={{0,1},{1,2},{2,3},{3,4},{4,5},{5,6},{6,7},{7,8},{8,9},{9,10},{10,1... | collective-permute-start | bytes 3538952 | tf_op jit(solution)/shard_map/ppermute | solution.py:17
  503.8 634.6 %collective-permute-start.13 = (bf16[2,384,768]{2,1,0:T(8,128)(2,1)}, bf16[2,384,768]{2,1,0:T(8,128)(2,1)}, u32[]{:S(2)}, u32[]{:S(2)}) collective-permute-start(bf16[2,384,768]{2,1,0:T(8,128)(2,1)} %get-tuple-element.292), channel_id=1, source_target_pairs={{0,3},{1,4},{2,5},{3,6},{4,7},{5,8},{6,9},{7,10},{8,11},{9,12},{10... | collective-permute-start | bytes 3538952 | tf_op jit(solution)/shard_map/ppermute | solution.py:17
  505.8 632.7 %collective-permute-start.14 = (bf16[2,384,768]{2,1,0:T(8,128)(2,1)}, bf16[2,384,768]{2,1,0:T(8,128)(2,1)}, u32[]{:S(2)}, u32[]{:S(2)}) collective-permute-start(bf16[2,384,768]{2,1,0:T(8,128)(2,1)} %get-tuple-element.291), channel_id=1, source_target_pairs={{0,4},{1,5},{2,6},{3,7},{4,8},{5,9},{6,10},{7,11},{8,12},{9,13},{1... | collective-permute-start | bytes 3538952 | tf_op jit(solution)/shard_map/ppermute | solution.py:17
  517.6 141.5 %copy-start.3 = (bf16[2,384,768]{2,1,0:T(8,128)(2,1)S(1)}, bf16[2,384,768]{2,1,0:T(8,128)(2,1)}, u32[]{:S(2)}) copy-start(bf16[2,384,768]{2,1,0:T(8,128)(2,1)} %get-tuple-element.296) | copy-start | bytes 3538948
  564.8 573.7 %collective-permute-start.15 = (bf16[2,384,768]{2,1,0:T(8,128)(2,1)}, bf16[2,384,768]{2,1,0:T(8,128)(2,1)}, u32[]{:S(2)}, u32[]{:S(2)}) collective-permute-start(bf16[2,384,768]{2,1,0:T(8,128)(2,1)} %get-tuple-element.297), channel_id=1, source_target_pairs={{0,5},{1,6},{2,7},{3,8},{4,9},{5,10},{6,11},{7,12},{8,13},{9,14},{... | collective-permute-start | bytes 3538952 | tf_op jit(solution)/shard_map/ppermute | solution.py:17
  657.2 481.3 %collective-permute-start.8 = (bf16[2,384,768]{2,1,0:T(8,128)(2,1)}, bf16[2,384,768]{2,1,0:T(8,128)(2,1)}, u32[]{:S(2)}, u32[]{:S(2)}) collective-permute-start(bf16[2,384,768]{2,1,0:T(8,128)(2,1)} %get-tuple-element.290), channel_id=1, source_target_pairs={{5,0},{6,1},{7,2},{8,3},{9,4},{10,5},{11,6},{12,7},{13,8},{14,9},{... | collective-permute-start | bytes 3538952 | tf_op jit(solution)/shard_map/ppermute | solution.py:17
  659.1 479.4 %collective-permute-start.9 = (bf16[2,384,768]{2,1,0:T(8,128)(2,1)S(1)}, bf16[2,384,768]{2,1,0:T(8,128)(2,1)}, u32[]{:S(2)}, u32[]{:S(2)}) collective-permute-start(bf16[2,384,768]{2,1,0:T(8,128)(2,1)S(1)} %copy-done.3), channel_id=1, source_target_pairs={{4,0},{5,1},{6,2},{7,3},{8,4},{9,5},{10,6},{11,7},{12,8},{13,9},{1... | collective-permute-start | bytes 3538952 | tf_op jit(solution)/shard_map/ppermute | solution.py:17
  (4 other events, 68.5 us)
Sparse Core Ops, SparseCore 0:
  36.7 17.2 all-gather.1
  517.8 54.9 reduce-scatter.1
where the time goes:
time: 1170 us; the launch traced here: 1150 us
  blocking collectives  473 us (40%)
  waiting for transfers between devices  374 us (32%)
  starting transfers between devices  100 us (9%)
  matrix products  82.9 us (7%)
  other arithmetic  58.8 us (5%)
  local copies, waits for them, and re-layouts  50.1 us (4%)
  between operations  14.4 us (1%)
    psum x1, blocking collectives, body(): weight_grad = lax.psum(weight_part, 'tile').astype(jnp.bfloat16)  473 us
    ppermute x16, waiting for transfers between devices, from_behind(): lax.ppermute(value, axis, [(source, source + steps) for source in range(i...  374 us
    ppermute x16, starting transfers between devices, from_behind(): lax.ppermute(value, axis, [(source, source + steps) for source in range(i...  99.9 us
  transfers between devices with their start and end apart: 18, of which 6 were waited for; matrix products, arithmetic and copies ran while one was open for 4% of the time, Pallas kernels for 0%

commit v1 on v0

v1 whole, which is shorter than its diff:
```python
import functools
import math

import jax
import jax.numpy as jnp
from jax import lax
from jax.experimental import pallas as pl
from jax.experimental.pallas import tpu as pltpu
from jax.sharding import PartitionSpec as P

MESH = pl.DeviceIdType.MESH
HEAD_DIM = 128
TILE = 384
NB = 5
HEADS = 6
RING = 8
RINGS = 8
FEAT = HEADS * HEAD_DIM
GRP = 4
DBLK = 384
DOUT = GRP * DBLK
FACTOR = 1.0 / math.sqrt(HEAD_DIM)
BF16 = jnp.bfloat16
F32 = jnp.float32
VMEM_LIMIT = 56 * 1024 * 1024


def whereabouts():
    tile = lax.axis_index("tile")
    grp = lax.axis_index("grp")
    z = tile % RING
    ring = tile // RING
    core = grp % 2
    idle = 3 - 2 * core
    return tile, grp, z, ring, core, idle


def owns(z, idle):
    return z % 4 != idle


def head_at(z, idle):
    zz = z % 4
    return (z // 4) * 3 + zz - jnp.where(zz > idle, 1, 0)


def place_of(head, idle):
    hh = head % 3
    return (head // 3) * 4 + hh + jnp.where(hh >= idle, 1, 0)


def head_cols(head):
    return pl.ds(pl.multiple_of(head * HEAD_DIM, HEAD_DIM), HEAD_DIM)


def remote(src, dst, send_sem, recv_sem, **where):
    return pltpu.make_async_remote_copy(
        src_ref=src,
        dst_ref=dst,
        send_sem=send_sem,
        recv_sem=recv_sem,
        device_id=where,
        device_id_type=MESH,
    )


def signal(barrier, **where):
    pl.semaphore_signal(barrier, inc=1, device_id=where, device_id_type=MESH)


def greet_ring(barrier, tile, z, ring):
    @pl.loop(1, RING)
    def _(s):
        signal(barrier, tile=tile - z + (z + s) % RING)

    @pl.when(ring > 0)
    def _():
        signal(barrier, tile=tile - RING)

    @pl.when(ring < RINGS - 1)
    def _():
        signal(barrier, tile=tile + RING)


def ring_edges(ring):
    return jnp.where(ring > 0, 1, 0) + jnp.where(ring < RINGS - 1, 1, 0)


def inbound_kernel(
    nb, q, k, v, cot, w,
    nb8, q8, k16, v16, g8, cotf,
    cot_s, g_loc, ssem, rsem, lsem, csend, crecv, clocal, hsend, hrecv,
):
    tile, grp, z, ring, core, idle = whereabouts()
    base = tile - z
    mine = owns(z, idle)
    barrier = pltpu.get_barrier_semaphore()
    greet_ring(barrier, tile, z, ring)
    other_core = grp + 1 - 2 * core
    other_y = (grp + 2) % GRP
    signal(barrier, grp=other_core)
    signal(barrier, grp=other_y)
    pl.semaphore_wait(barrier, RING - 1 + 2 + ring_edges(ring))

    to_y = remote(cot, cot_s.at[grp], csend.at[0], crecv.at[0], grp=other_y)
    to_core = remote(cot, cot_s.at[grp], csend.at[1], crecv.at[1], grp=other_core)
    to_y.start()
    to_core.start()
    keep = pltpu.make_async_copy(cot, cot_s.at[grp], clocal.at[0])
    keep.start()

    def ends(kind, at):
        cols = head_cols(head_at(at, idle))
        if kind == 0:
            return k.at[:, cols], k16.at[z + 4]
        if kind == 1:
            return v.at[:, cols], v16.at[z + 4]
        if kind == 2:
            return q.at[:, cols], q8.at[z]
        if kind == 3:
            return g_loc.at[head_at(at, idle)], g8.at[z]
        return nb.at[0], nb8.at[z]

    def send(kind, s):
        at = (z + s) % RING
        src, dst = ends(kind, at)
        return remote(src, dst, ssem.at[kind, s], rsem.at[kind, z], tile=base + at)

    def keep_own(kind):
        src, dst = ends(kind, z)
        return pltpu.make_async_copy(src, dst, lsem.at[kind])

    def arrived(kind, at):
        dst = (k16.at[at + 4], v16.at[at + 4], q8.at[at], g8.at[at], nb8.at[at])[kind]
        return remote(dst, dst, ssem.at[kind, 0], rsem.at[kind, at], tile=base + at)

    for kinds in ((0, 1), (2, 4)):
        @pl.loop(1, RING)
        def _(s):
            @pl.when(owns(z + s, idle))
            def _():
                for kind in kinds:
                    send(kind, s).start()

    @pl.when(mine)
    def _():
        for kind in (0, 1, 2, 4):
            keep_own(kind).start()

    remote(cot, cot_s.at[other_y], csend.at[0], crecv.at[0], grp=other_y).wait_recv()
    on = remote(cot_s.at[other_y], cot_s.at[other_y], csend.at[2], crecv.at[2], grp=other_core)
    on.start()
    far = (other_core + 2) % GRP
    remote(cot, cot_s.at[other_core], csend.at[1], crecv.at[1], grp=other_core).wait_recv()
    remote(cot, cot_s.at[far], csend.at[2], crecv.at[2], grp=other_core).wait_recv()
    keep.wait()
    out = pltpu.make_async_copy(cot_s, cotf, clocal.at[1])
    out.start()

    @pl.loop(0, RING)
    def _(s):
        at = (z + s) % RING

        @pl.when(owns(at, idle))
        def _():
            head = head_at(at, idle)
            rows = head_cols(head)
            total = None
            for b in range(GRP):
                part = lax.dot_general(
                    cot_s[b], w[rows, b * DBLK:(b + 1) * DBLK],
                    (((1,), (1,)), ((), ())), preferred_element_type=F32,
                )
                total = part if total is None else total + part
            g_loc[head] = total.astype(BF16)

            @pl.when(s > 0)
            def _():
                send(3, s).start()

            @pl.when(s == 0)
            def _():
                keep_own(3).start()

    def hop(kind, at, start):
        buf = (k16, v16)[kind]

        @pl.when((at >= 4) & (ring < RINGS - 1))
        def _():
            c = remote(buf.at[at + 4], buf.at[at - 4], hsend.at[kind, at], hrecv.at[kind, at],
                       tile=tile + RING)
            if start:
                c.start()
            else:
                c.wait_send()

        @pl.when((at < 4) & (ring > 0))
        def _():
            c = remote(buf.at[at + 4], buf.at[at + 12], hsend.at[kind, at], hrecv.at[kind, at],
                       tile=tile - RING)
            if start:
                c.start()
            else:
                c.wait_send()

    def hop_arrived(kind, at):
        buf = (k16, v16)[kind]

        @pl.when((at >= 4) & (ring > 0))
        def _():
            remote(buf.at[at - 4], buf.at[at - 4], hsend.at[kind, at], hrecv.at[kind, at],
                   tile=tile - RING).wait_recv()

        @pl.when((at < 4) & (ring < RINGS - 1))
        def _():
            remote(buf.at[at + 12], buf.at[at + 12], hsend.at[kind, at], hrecv.at[kind, at],
                   tile=tile + RING).wait_recv()

    @pl.when(mine)
    def _():
        for kind in (0, 1):
            keep_own(kind).wait()
            hop(kind, z, True)

        @pl.loop(1, RING)
        def _(s):
            at = (z + RING - s) % RING
            for kind in (0, 1):
                arrived(kind, at).wait_recv()
                hop(kind, at, True)

        for kind in (2, 3, 4):
            keep_own(kind).wait()

        @pl.loop(1, RING)
        def _(s):
            at = (z + RING - s) % RING
            for kind in (2, 3, 4):
                arrived(kind, at).wait_recv()

        @pl.loop(0, RING)
        def _(at):
            for kind in (0, 1):
                hop_arrived(kind, at)
                hop(kind, at, False)

    @pl.loop(1, RING)
    def _(s):
        @pl.when(owns(z + s, idle))
        def _():
            for kind in range(5):
                send(kind, s).wait_send()

    to_y.wait_send()
    to_core.wait_send()
    on.wait_send()
    out.wait()


def inbound(nb, q, k, v, cot, w):
    any_space = pl.BlockSpec(memory_space=pl.ANY)
    vmem = pl.BlockSpec(memory_space=pltpu.VMEM)
    dma = pltpu.SemaphoreType.DMA
    return pl.pallas_call(
        inbound_kernel,
        out_shape=(
            jax.ShapeDtypeStruct((RING, 8, 128), jnp.int32),
            jax.ShapeDtypeStruct((RING, TILE, HEAD_DIM), BF16),
            jax.ShapeDtypeStruct((2 * RING, TILE, HEAD_DIM), BF16),
            jax.ShapeDtypeStruct((2 * RING, TILE, HEAD_DIM), BF16),
            jax.ShapeDtypeStruct((RING, TILE, HEAD_DIM), BF16),
            jax.ShapeDtypeStruct((GRP, TILE, DBLK), BF16),
        ),
        in_specs=[any_space, any_space, any_space, any_space, vmem, vmem],
        out_specs=(any_space,) * 6,
        scratch_shapes=[
            pltpu.VMEM((GRP, TILE, DBLK), BF16),
            pltpu.VMEM((HEADS, TILE, HEAD_DIM), BF16),
            dma((5, RING)),
            dma((5, RING)),
            dma((5,)),
            dma((3,)),
            dma((3,)),
            dma((2,)),
            dma((2, RING)),
            dma((2, RING)),
        ],
        compiler_params=pltpu.CompilerParams(
            collective_id=0, has_side_effects=True, vmem_limit_bytes=VMEM_LIMIT
        ),
        name="inbound",
    )(nb, q, k, v, cot, w)


def attention_kernel(
    nb, tokens, q_ref, g_ref, k_ref, v_ref,
    att_ref, dq_ref, dko, dvo, dkh, dvh,
    acck, accv, e_scr,
):
    tile, grp, z, ring, core, idle = whereabouts()
    r = pl.program_id(0)

    @pl.when(owns(z, idle))
    def _():
        @pl.when(r == 0)
        def _():
            acck[...] = jnp.zeros_like(acck)
            accv[...] = jnp.zeros_like(accv)

        live = jnp.int32(0)
        for j in range(NB):
            live += jnp.where(nb[r, 0, j] >= 0, 1, 0)
        q = q_ref[0]
        g = g_ref[0]
        rows = lax.broadcasted_iota(jnp.int32, (TILE, TILE), 0)

        def local(j):
            return nb[r, 0, j] - ring * RING + 4

        def scores(j, top):
            s = lax.dot_general(
                k_ref[local(j)], q, (((1,), (1,)), ((), ())), preferred_element_type=F32
            )
            s = jnp.where(rows < tokens[nb[r, 0, j]], s, F32(-1e30))
            e_scr[j] = s
            return jnp.maximum(top, jnp.max(s, axis=0, keepdims=True))

        top = lax.fori_loop(0, live, scores, jnp.full((1, TILE), -1e30, F32))

        def exponents(j, total):
            e = jnp.exp2((e_scr[j] - top) * F32(FACTOR * math.log2(math.e)))
            e_scr[j] = e
            return total + jnp.sum(e, axis=0, keepdims=True)

        total = lax.fori_loop(0, live, exponents, jnp.zeros((1, TILE), F32))
        inverse = 1.0 / total

        def forward(j, out):
            p = e_scr[j] * inverse
            e_scr[j] = p
            return out + lax.dot_general(
                v_ref[local(j)], p.astype(BF16), (((0,), (0,)), ((), ())),
                preferred_element_type=F32,
            )

        out = lax.fori_loop(0, live, forward, jnp.zeros((HEAD_DIM, TILE), F32))
        att_ref[0] = out.T.astype(BF16)
        delta = jnp.sum(out * g.astype(F32).T, axis=0, keepdims=True)

        def backward(j, dq):
            at = local(j)
            p = e_scr[j]
            kk = k_ref[at]
            gp = lax.dot_general(
                v_ref[at], g, (((1,), (1,)), ((), ())), preferred_element_type=F32
            )
            ds = (p * (gp - delta) * F32(FACTOR)).astype(BF16)
            accv[at] += jnp.dot(p.astype(BF16), g, preferred_element_type=F32)
            acck[at] += jnp.dot(ds, q, preferred_element_type=F32)
            return dq + lax.dot_general(
                kk, ds, (((0,), (0,)), ((), ())), preferred_element_type=F32
            )

        dq = lax.fori_loop(0, live, backward, jnp.zeros((HEAD_DIM, TILE), F32))
        dq_ref[0] = dq.T.astype(BF16)

        @pl.when(r == RING - 1)
        def _():
            dko[...] = acck[4:12]
            dvo[...] = accv[4:12]
            dkh[0:4] = acck[0:4].astype(BF16)
            dkh[4:8] = acck[12:16].astype(BF16)
            dvh[0:4] = accv[0:4].astype(BF16)
            dvh[4:8] = accv[12:16].astype(BF16)


def attention(nb8, tokens, q8, g8, k16, v16):
    smem = pl.BlockSpec(memory_space=pltpu.SMEM)
    one = pl.BlockSpec((1, TILE, HEAD_DIM), lambda i: (i, 0, 0))

    def whole(n):
        return pl.BlockSpec((n, TILE, HEAD_DIM), lambda i: (0, 0, 0))

    def shape(n, dtype):
        return jax.ShapeDtypeStruct((n, TILE, HEAD_DIM), dtype)

    return pl.pallas_call(
        attention_kernel,
        grid=(RING,),
        out_shape=(
            shape(RING, BF16), shape(RING, BF16), shape(RING, F32), shape(RING, F32),
            shape(RING, BF16), shape(RING, BF16),
        ),
        in_specs=[smem, smem, one, one, whole(2 * RING), whole(2 * RING)],
        out_specs=(one, one, whole(RING), whole(RING), whole(RING), whole(RING)),
        scratch_shapes=[
            pltpu.VMEM((2 * RING, TILE, HEAD_DIM), F32),
            pltpu.VMEM((2 * RING, TILE, HEAD_DIM), F32),
            pltpu.VMEM((NB, TILE, TILE), F32),
        ],
        compiler_params=pltpu.CompilerParams(vmem_limit_bytes=VMEM_LIMIT),
        name="attention",
    )(nb8, tokens, q8, g8, k16, v16)


XROWS = FEAT // 4
YROWS = XROWS // 2
ZROWS = YROWS // 2
ZCOLS = DOUT // 4
HALF = DOUT // 2


def outbound_kernel(
    att8, dq8, dko, dvo, dkh, dvh, cot_s, w,
    bo, dq, dk, dv, dw,
    att_s, hk, hv, dkb, dvb, dwp, xl, xs, xacc, ys, yl, zs, zl, fin, pos, pol, own, ybs, ybl,
    ssem, rsem, lsem, hsend, hrecv, xsend, xrecv, ysend, yrecv, zsend, zrecv, gsend, grecv,
):
    tile, grp, z, ring, core, idle = whereabouts()
    base = tile - z
    mine = owns(z, idle)
    head = head_at(z, idle)
    x = ring % 4
    y = ring // 4
    right = tile - x * RING + (x + 1) % 4 * RING
    left = tile - x * RING + (x + 3) % 4 * RING
    y_pair = tile + 32 - 64 * y
    other_core = grp + 1 - 2 * core
    other_y = (grp + 2) % GRP
    y_hi = grp // 2

    barrier = pltpu.get_barrier_semaphore()
    greet_ring(barrier, tile, z, ring)
    signal(barrier, tile=right)
    signal(barrier, tile=left)
    signal(barrier, tile=y_pair)
    signal(barrier, grp=other_core)
    signal(barrier, grp=other_y)
    pl.semaphore_wait(barrier, RING - 1 + 5 + ring_edges(ring))

    def ends(kind, at, h):
        src = (att8, dq8, dkb, dvb)[kind].at[at]
        dst = (att_s, dq, dk, dv)[kind].at[:, head_cols(h)]
        return src, dst

    def send(kind, s):
        at = (z + s) % RING
        src, dst = ends(kind, at, head)
        return remote(src, dst, ssem.at[kind, s], rsem.at[kind, head], tile=base + at)

    def keep_own(kind):
        src, dst = ends(kind, z, head)
        return pltpu.make_async_copy(src, dst, lsem.at[kind])

    def start_all(kind):
        keep_own(kind).start()

        @pl.loop(1, RING)
        def _(s):
            send(kind, s).start()

    def wait_all(kind):
        @pl.loop(0, HEADS)
        def _(h):
            at = place_of(h, idle)
            src, dst = ends(kind, z, h)

            @pl.when(at != z)
            def _():
                remote(src, dst, ssem.at[kind, 0], rsem.at[kind, h], tile=base + at).wait_recv()

        @pl.when(mine)
        def _():
            keep_own(kind).wait()

    def sent_all(kind):
        @pl.loop(1, RING)
        def _(s):
            send(kind, s).wait_send()

    def halo(kind, up):
        src, dst = ((dkh, hk), (dvh, hv))[kind]
        if up:
            return remote(src.at[pl.ds(4, 4)], dst.at[pl.ds(0, 4)], hsend.at[kind, 1],
                          hrecv.at[kind, 0], tile=tile + RING)
        return remote(src.at[pl.ds(0, 4)], dst.at[pl.ds(4, 4)], hsend.at[kind, 0],
                      hrecv.at[kind, 1], tile=tile - RING)

    @pl.when(mine)
    def _():
        start_all(0)
        for kind in (0, 1):
            @pl.when(ring > 0)
            def _():
                halo(kind, False).start()

            @pl.when(ring < RINGS - 1)
            def _():
                halo(kind, True).start()

        start_all(1)

    wait_all(0)

    @pl.loop(0, HEADS)
    def _(h):
        rows = head_cols(h)
        turned = att_s[:, rows].T
        for b in range(GRP):
            dwp[rows, b * DBLK:(b + 1) * DBLK] = jnp.dot(
                turned, cot_s[b], preferred_element_type=F32
            ).astype(BF16)

    def xblock(i):
        return pl.ds(pl.multiple_of(i % 4 * XROWS, XROWS), XROWS)

    half_a, half_b = pl.ds(0, HALF), pl.ds(HALF, HALF)
    rel_a = remote(dwp.at[xblock(x + 2), half_a], xl.at[0], xsend.at[0], xrecv.at[0], tile=left)
    rel_b = remote(dwp.at[xblock(x + 2), half_b], xl.at[1], xsend.at[1], xrecv.at[1], tile=right)
    one_a = remote(dwp.at[xblock(x + 1), half_a], xl.at[2], xsend.at[2], xrecv.at[2], tile=right)
    one_b = remote(dwp.at[xblock(x + 3), half_b], xl.at[3], xsend.at[3], xrecv.at[3], tile=left)
    sum_a = remote(xs.at[0], xl.at[4], xsend.at[4], xrecv.at[4], tile=left)
    sum_b = remote(xs.at[1], xl.at[5], xsend.at[5], xrecv.at[5], tile=right)
    for c in (rel_a, rel_b, one_a, one_b):
        c.start()

    def projected(b):
        cols = pl.ds(pl.multiple_of(b * DBLK, DBLK), DBLK)
        return jnp.dot(att_s[...], w[:, cols], preferred_element_type=F32)

    @pl.loop(0, 2)
    def _(yy):
        pos[yy] = projected(yy * 2 + 1 - core)

    to_core = remote(pos, pol, gsend.at[0], grecv.at[0], grp=other_core)
    to_core.start()

    @pl.loop(0, 2)
    def _(yy):
        own[yy] = projected(yy * 2 + core)

    rel_a.wait_recv()
    xs[0] = (xl[0].astype(F32) + dwp[xblock(x + 3), half_a].astype(F32)).astype(BF16)
    sum_a.start()
    rel_b.wait_recv()
    xs[1] = (xl[1].astype(F32) + dwp[xblock(x + 1), half_b].astype(F32)).astype(BF16)
    sum_b.start()

    to_core.wait_recv()
    ybs[...] = (own[1 - y_hi] + pol[1 - y_hi]).astype(BF16)
    to_y = remote(ybs, ybl, gsend.at[1], grecv.at[1], grp=other_y)
    to_y.start()

    @pl.when(mine)
    def _():
        for kind in (0, 1):
            full, got, out = ((dko, hk, dkb), (dvo, hv, dvb))[kind]

            def back(up, first, has):
                @pl.when(has)
                def _():
                    halo(kind, up).wait_recv()

                    @pl.loop(first, first + 4)
                    def _(i):
                        out[i] = (full[i] + got[i].astype(F32)).astype(BF16)

                @pl.when(jnp.logical_not(has))
                def _():
                    @pl.loop(first, first + 4)
                    def _(i):
                        out[i] = full[i].astype(BF16)

            back(True, 0, ring > 0)
            back(False, 4, ring < RINGS - 1)
            start_all(2 + kind)

    one_a.wait_recv()
    sum_a.wait_recv()
    xacc[:, :HALF] = (
        dwp[xblock(x), :HALF].astype(F32) + xl[2].astype(F32) + xl[4].astype(F32)
    )
    one_b.wait_recv()
    sum_b.wait_recv()
    xacc[:, HALF:] = (
        dwp[xblock(x), HALF:].astype(F32) + xl[3].astype(F32) + xl[5].astype(F32)
    )
    my_rows = pl.ds(pl.multiple_of(y * YROWS, YROWS), YROWS)
    ys[...] = xacc[pl.ds(pl.multiple_of((1 - y) * YROWS, YROWS), YROWS), :].astype(BF16)
    y_sum = remote(ys, yl, ysend.at[0], yrecv.at[0], tile=y_pair)
    y_sum.start()
    y_sum.wait_recv()
    zs[...] = (xacc[my_rows, :] + yl[...].astype(F32)).astype(BF16)

    def zpart(at):
        return (
            pl.ds(pl.multiple_of(at // 4 * ZROWS, ZROWS), ZROWS),
            pl.ds(pl.multiple_of(at % 4 * ZCOLS, ZCOLS), ZCOLS),
        )

    def z_sum(s):
        at = (z + s) % RING
        return remote(zs.at[zpart(at)], zl.at[z], zsend.at[0, s], zrecv.at[0, z], tile=base + at)

    @pl.loop(1, RING)
    def _(s):
        z_sum(s).start()

    to_y.wait_recv()
    bo[...] = (own[y_hi] + pol[y_hi] + ybl[...].astype(F32)).astype(BF16)

    def z_sum_got(at):
        return remote(zl.at[at], zl.at[at], zsend.at[0, 0], zrecv.at[0, at], tile=base + at)

    rows, cols = zpart(z)
    total = zs[rows, cols].astype(F32)
    for s in range(1, RING):
        at = (z + s) % RING
        z_sum_got(at).wait_recv()
        total += zl[at].astype(F32)
    fin[...] = total.astype(BF16)

    slab = x * XROWS + y * YROWS

    def home(at):
        rows = pl.ds(pl.multiple_of(slab + at // 4 * ZROWS, ZROWS), ZROWS)
        return dw.at[rows, zpart(at)[1]]

    def z_all(s):
        at = (z + s) % RING
        return remote(fin, home(z), zsend.at[1, s], zrecv.at[1, z], tile=base + at)

    @pl.loop(1, RING)
    def _(s):
        z_all(s).start()

    kept = pltpu.make_async_copy(fin, home(z), lsem.at[4])
    kept.start()
    kept.wait()

    @pl.loop(1, RING)
    def _(s):
        at = (z + s) % RING
        remote(fin, home(at), zsend.at[1, 0], zrecv.at[1, at], tile=base + at).wait_recv()

    def yslab(yy):
        return dw.at[pl.ds(pl.multiple_of(x * XROWS + yy * YROWS, YROWS), YROWS), :]

    y_all = remote(yslab(y), yslab(y), ysend.at[1], yrecv.at[1], tile=y_pair)
    y_all.start()
    remote(yslab(1 - y), yslab(1 - y), ysend.at[1], yrecv.at[1], tile=y_pair).wait_recv()

    def xslab(i, part):
        return dw.at[xblock(i), (half_a, half_b)[part]]

    def x_all(i, part, slot, to):
        return remote(xslab(i, part), xslab(i, part), xsend.at[slot], xrecv.at[slot], tile=to)

    outs = [
        x_all(x, 0, 6, right), x_all(x, 1, 7, left), x_all(x, 1, 8, right), x_all(x, 0, 9, left)
    ]
    for c in outs:
        c.start()
    x_all(x + 3, 0, 6, left).wait_recv()
    pass_a = x_all(x + 3, 0, 10, right)
    pass_a.start()
    x_all(x + 1, 1, 7, right).wait_recv()
    pass_b = x_all(x + 1, 1, 11, left)
    pass_b.start()
    x_all(x + 3, 1, 8, left).wait_recv()
    x_all(x + 1, 0, 9, right).wait_recv()
    x_all(x + 2, 0, 10, left).wait_recv()
    x_all(x + 2, 1, 11, right).wait_recv()

    for kind in (1, 2, 3):
        wait_all(kind)

    @pl.when(mine)
    def _():
        for kind in range(4):
            sent_all(kind)
        for kind in (0, 1):
            @pl.when(ring > 0)
            def _():
                halo(kind, False).wait_send()

            @pl.when(ring < RINGS - 1)
            def _():
                halo(kind, True).wait_send()

    for c in (rel_a, rel_b, one_a, one_b, sum_a, sum_b, to_core, to_y, y_sum, y_all, pass_a, pass_b):
        c.wait_send()
    for c in outs:
        c.wait_send()

    @pl.loop(1, RING)
    def _(s):
        z_sum(s).wait_send()
        z_all(s).wait_send()


def outbound(att8, dq8, dko, dvo, dkh, dvh, cotf, w):
    any_space = pl.BlockSpec(memory_space=pl.ANY)
    vmem = pl.BlockSpec(memory_space=pltpu.VMEM)
    dma = pltpu.SemaphoreType.DMA
    grad = jax.ShapeDtypeStruct((TILE, FEAT), BF16)
    return pl.pallas_call(
        outbound_kernel,
        out_shape=(
            jax.ShapeDtypeStruct((TILE, DBLK), BF16), grad, grad, grad,
            jax.ShapeDtypeStruct((FEAT, DOUT), BF16),
        ),
        in_specs=[any_space, any_space, vmem, vmem, any_space, any_space, vmem, vmem],
        out_specs=(vmem, any_space, any_space, any_space, any_space),
        scratch_shapes=[
            pltpu.VMEM((TILE, FEAT), BF16),
            pltpu.VMEM((RING, TILE, HEAD_DIM), BF16),
            pltpu.VMEM((RING, TILE, HEAD_DIM), BF16),
            pltpu.VMEM((RING, TILE, HEAD_DIM), BF16),
            pltpu.VMEM((RING, TILE, HEAD_DIM), BF16),
            pltpu.VMEM((FEAT, DOUT), BF16),
            pltpu.VMEM((6, XROWS, HALF), BF16),
            pltpu.VMEM((2, XROWS, HALF), BF16),
            pltpu.VMEM((XROWS, DOUT), F32),
            pltpu.VMEM((YROWS, DOUT), BF16),
            pltpu.VMEM((YROWS, DOUT), BF16),
            pltpu.VMEM((YROWS, DOUT), BF16),
            pltpu.VMEM((RING, ZROWS, ZCOLS), BF16),
            pltpu.VMEM((ZROWS, ZCOLS), BF16),
            pltpu.VMEM((2, TILE, DBLK), F32),
            pltpu.VMEM((2, TILE, DBLK), F32),
            pltpu.VMEM((2, TILE, DBLK), F32),
            pltpu.VMEM((TILE, DBLK), BF16),
            pltpu.VMEM((TILE, DBLK), BF16),
            dma((4, RING)),
            dma((4, HEADS)),
            dma((5,)),
            dma((2, 2)),
            dma((2, 2)),
            dma((12,)),
            dma((12,)),
            dma((2,)),
            dma((2,)),
            dma((2, RING)),
            dma((2, RING)),
            dma((2,)),
            dma((2,)),
        ],
        compiler_params=pltpu.CompilerParams(
            collective_id=1, has_side_effects=True, vmem_limit_bytes=VMEM_LIMIT
        ),
        name="outbound",
    )(att8, dq8, dko, dvo, dkh, dvh, cotf, w)


def body(query_tokens, key_tokens, value_tokens, w_out, cotangent, neighbours, tile_tokens):
    nb = jnp.pad(neighbours.reshape(1, 1, NB), ((0, 0), (0, 7), (0, 128 - NB)), constant_values=-1)
    nb8, q8, k16, v16, g8, cotf = inbound(
        nb, query_tokens, key_tokens, value_tokens, cotangent, w_out
    )
    att8, dq8, dko, dvo, dkh, dvh = attention(nb8, tile_tokens, q8, g8, k16, v16)
    return outbound(att8, dq8, dko, dvo, dkh, dvh, cotf, w_out)


def solution(mesh):
    placed = (
        P("tile", "grp"),
        P("tile", "grp"),
        P("tile", "grp"),
        P("grp", None),
        P("tile", "grp"),
        P("tile", None),
        P(),
    )
    return jax.shard_map(
        body,
        mesh=mesh,
        in_specs=placed,
        out_specs=(
            P("tile", "grp"),
            P("tile", "grp"),
            P("tile", "grp"),
            P("tile", "grp"),
            P("grp", None),
        ),
        check_vma=False,
    )
```

time: 1170 us -> 247 us (0.21); the launches traced: 1150 us -> 245 us
  blocking collectives: 473 us -> 0 us
  waiting for transfers between devices: 374 us -> 0 us
  Pallas kernels: 0 us -> 236 us
  starting transfers between devices: 100 us -> 0 us
  matrix products: 82.9 us -> 0 us
  other arithmetic: 58.8 us -> 0 us
  local copies, waits for them, and re-layouts: 50.1 us -> 8.16 us
  between operations: 14.4 us -> 0.67 us
    psum x1 -> x0, blocking collectives: 473 us -> none  [body(): weight_grad = lax.psum(weight_part, 'tile').astype(jnp.bfloat16)]
    ppermute x16 -> x0, waiting for transfers between devices: 374 us -> none  [from_behind(): lax.ppermute(value, axis, [(source, source + steps) for source in range(i...]
    pallas_call x0 -> x3, Pallas kernels: none -> 236 us  [the longest x1 123 us: outbound(): pl.pallas_call(outbound_kernel, out_shape=(jax.ShapeDtypeStruct((TILE, DB...]
    ppermute x16 -> x0, starting transfers between devices: 99.9 us -> none  [from_behind(): lax.ppermute(value, axis, [(source, source + steps) for source in range(i...]
    dot_general x39 -> x0, matrix products: 82.9 us -> none  [the longest x6 16.8 us: head_pass(): lax.dot_general(weights, grad_rows, (((0,), (0,)), ((), ())), preferred_e...]
    scatter-add x2 -> x0, other arithmetic: 26.7 us -> none  [the longest x1 13.4 us: tile_step(): value_buffer.at[slot_index].add(dv_rows.reshape(-1, TILE, width_here))]
    convert_element_type x8 -> x0, other arithmetic: 13 us -> none  [the longest x1 6.05 us: body(): value_total.astype(jnp.bfloat16)]
  transfers between devices with their start and end apart: 18 -> 0, of which waited for: 6 -> 0; matrix products, arithmetic and copies ran while one was open for 4% -> 0% of each run, Pallas kernels for 0% -> 0%
where the time goes in v1:
time: 247 us; the launch traced here: 245 us
  Pallas kernels  236 us (96%)
  local copies, waits for them, and re-layouts  8.16 us (3%)
    pallas_call x1, Pallas kernels, outbound(): pl.pallas_call(outbound_kernel, out_shape=(jax.ShapeDtypeStruct((TILE, DB...  123 us
    pallas_call x1, Pallas kernels, inbound(): pl.pallas_call(inbound_kernel, out_shape=(jax.ShapeDtypeStruct((RING, 8,...  69.2 us
    pallas_call x1, Pallas kernels, attention(): pl.pallas_call(attention_kernel, grid=(RING,), out_shape=(shape(RING, BF1...  43.8 us
    unnamed x11, local copies, waits for them, and re-layouts  6.91 us

profile of v1, /device:TPU:24, one launch (start us, length us, event | category | flops | bytes accessed | tf_op | source)
XLA Modules:
  0.0 244.9 jit_solution(12535161846382960021)
XLA Ops:
  0.6 1.3 pad.4.nb
  1.9 69.2 %inbound.1 = (s32[8,8,128]{2,1,0:T(8,128)}, bf16[8,384,128]{2,1,0:T(8,128)(2,1)}, bf16[16,384,128]{2,1,0:T(8,128)(2,1)}, bf16[16,384,128]{2,1,0:T(8,128)(2,1)}, ...) custom-call(s32[1,8,128]{2,1,0:T(8,128)} %pad.4.nb, bf16[384,768]{1,0:T(8,128)(2,1)} %q.1, bf16[384,768]{1,0:T(8,128)(2,1)} %k.1, ...), custom_call_target="tpu_custom_call" | custom-call | tf_op jit(solution)/shard_map/inbound/pallas_call | solution.py:264
  71.1 43.8 %attention.1 = (bf16[8,384,128]{2,1,0:T(8,128)(2,1)}, bf16[8,384,128]{2,1,0:T(8,128)(2,1)}, f32[8,384,128]{2,1,0:T(8,128)}, f32[8,384,128]{2,1,0:T(8,128)}, bf16...) custom-call(s32[8,8,128]{2,1,0:T(8,128)} %get-tuple-element.17.nb, s32[64]{0:T(128)} %tokens.1, ...), custom_call_target="tpu_custom_call" | custom-call | tf_op jit(solution)/shard_map/attention/pallas_call | solution.py:387
  114.9 123.1 %outbound.1 = (bf16[384,384]{1,0:T(8,128)(2,1)}, bf16[384,768]{1,0:T(8,128)(2,1)}, bf16[384,768]{1,0:T(8,128)(2,1)}, bf16[384,768]{1,0:T(8,128)(2,1)}, bf16[768,1536]{1,0:T(8,128)(2,1)}) custom-call(bf16[8,384,128]{2,1,0:T(8,128)(2,1)} %get-tuple-element.22.att8, bf16[8,384,128]{2,1,0:T(8,128)(2,1)} %get-tuple-element.23.dq8, ...), custom_call_target="tpu_custom_call" | custom-call | tf_op jit(solution)/shard_map/outbound/pallas_call | solution.py:707
  238.0 0.0 copy-start.2
  238.0 0.0 copy-start.1
  238.0 1.8 copy.17
  239.8 0.0 copy-start
  239.8 2.1 copy.18
  241.9 0.0 copy-done.2
  241.9 0.8 copy.19
  242.7 0.0 copy-done.1
  242.7 0.8 copy.20
  243.5 0.0 copy-done
  243.5 1.4 copy.21
Async XLA Ops:
  238.0 3.9 %copy-start.2 = (bf16[384,768]{1,0:T(8,128)(2,1)S(1)}, bf16[384,768]{1,0:T(8,128)(2,1)}, u32[]{:S(2)}) copy-start(bf16[384,768]{1,0:T(8,128)(2,1)} %get-tuple-element.36) | copy-start | bytes 1769476
  238.0 4.7 %copy-start.1 = (bf16[384,768]{1,0:T(8,128)(2,1)S(1)}, bf16[384,768]{1,0:T(8,128)(2,1)}, u32[]{:S(2)}) copy-start(bf16[384,768]{1,0:T(8,128)(2,1)} %get-tuple-element.37) | copy-start | bytes 1769476
  239.8 3.7 %copy-start = (bf16[768,1536]{1,0:T(8,128)(2,1)S(1)}, bf16[768,1536]{1,0:T(8,128)(2,1)}, u32[]{:S(2)}) copy-start(bf16[768,1536]{1,0:T(8,128)(2,1)} %get-tuple-element.38) | copy-start | bytes 7077892

commit v2 on v0

v2 whole, which is shorter than its diff:
```python
import math

import jax
import jax.numpy as jnp
from jax import lax
from jax.experimental import pallas as pl
from jax.experimental.pallas import tpu as pltpu
from jax.sharding import PartitionSpec as P

MESH = pl.DeviceIdType.MESH
HEAD_DIM = 128
TILE = 384
NB = 5
HEADS = 6
RING = 8
RINGS = 8
FEAT = HEADS * HEAD_DIM
GRP = 4
DBLK = 384
DOUT = GRP * DBLK
FACTOR = 1.0 / math.sqrt(HEAD_DIM)
BF16 = jnp.bfloat16
F32 = jnp.float32
VMEM_LIMIT = 56 * 1024 * 1024


def whereabouts():
    tile = lax.axis_index("tile")
    grp = lax.axis_index("grp")
    z = tile % RING
    ring = tile // RING
    core = grp % 2
    idle = 3 - 2 * core
    return tile, grp, z, ring, core, idle


def owns(z, idle):
    return z % 4 != idle


def head_at(z, idle):
    zz = z % 4
    return (z // 4) * 3 + zz - jnp.where(zz > idle, 1, 0)


def place_of(head, idle):
    hh = head % 3
    return (head // 3) * 4 + hh + jnp.where(hh >= idle, 1, 0)


def head_cols(head):
    return pl.ds(pl.multiple_of(head * HEAD_DIM, HEAD_DIM), HEAD_DIM)


def remote(src, dst, send_sem, recv_sem, **where):
    return pltpu.make_async_remote_copy(
        src_ref=src,
        dst_ref=dst,
        send_sem=send_sem,
        recv_sem=recv_sem,
        device_id=where,
        device_id_type=MESH,
    )


def signal(barrier, **where):
    pl.semaphore_signal(barrier, inc=1, device_id=where, device_id_type=MESH)


def greet_ring(barrier, tile, z, ring):
    @pl.loop(1, RING)
    def _(s):
        signal(barrier, tile=tile - z + (z + s) % RING)

    @pl.when(ring > 0)
    def _():
        signal(barrier, tile=tile - RING)

    @pl.when(ring < RINGS - 1)
    def _():
        signal(barrier, tile=tile + RING)


def ring_edges(ring):
    return jnp.where(ring > 0, 1, 0) + jnp.where(ring < RINGS - 1, 1, 0)

XROWS = FEAT // 4
YROWS = FEAT // 2
SROWS = FEAT // 8
ZROWS = SROWS // 2
ZCOLS = DOUT // 4
HALF = DOUT // 2
QUARTER = DOUT // 4
KEYS = NB * TILE
SHIFTS = tuple((dt, dh) for dt in (-1, 0, 1) for dh in (-1, 0, 1) if (dt, dh) != (0, 0))
LOG2E = math.log2(math.e)


def nt(a, b):
    return lax.dot_general(a, b, (((1,), (1,)), ((), ())), preferred_element_type=F32)


def tn(a, b):
    return lax.dot_general(a, b, (((0,), (0,)), ((), ())), preferred_element_type=F32)


def step_kernel(
    listed, tokens, q, k, v, cot, w,
    bo, dq, dk, dv, dw,
    nb_o, nb_v, nb_s, k16, v16, q8, g8, cot_s, g_loc, s_scr, p, vc, kc, ds_s, tmp, o_t, acck, accv,
    att8, dq8, att_s, hk, hv, hks, hvs, dkb, dvb,
    dwp, x1, x2, xs1, xs2, x_tot, y1s, y1l, y2l, y2, zs, zl, fin, pos, pol, own, ybs, ybl,
    ssem, rsem, lsem, csend, crecv, clocal, khsend, khrecv, osend, orecv, olocal, hsend, hrecv,
    xsend, xrecv, ysend, yrecv, zsend, zrecv, gsend, grecv,
):
    tile, grp, z, ring, core, idle = whereabouts()
    base = tile - z
    mine = owns(z, idle)
    my_head = head_at(z, idle)
    x = ring % 4
    y = ring // 4
    right = tile - x * RING + (x + 1) % 4 * RING
    left = tile - x * RING + (x + 3) % 4 * RING
    y_pair = tile + 32 - 64 * y
    other_core = grp + 1 - 2 * core
    other_y = (grp + 2) % GRP
    y_hi = grp // 2
    has_up = ring < RINGS - 1
    has_down = ring > 0

    barrier = pltpu.get_barrier_semaphore()
    greet_ring(barrier, tile, z, ring)
    for where in (right, left, y_pair):
        signal(barrier, tile=where)
    signal(barrier, grp=other_core)
    signal(barrier, grp=other_y)
    pl.semaphore_wait(barrier, RING - 1 + 5 + ring_edges(ring))

    cot_y = remote(cot, cot_s.at[grp], csend.at[0], crecv.at[0], grp=other_y)
    cot_core = remote(cot, cot_s.at[grp], csend.at[1], crecv.at[1], grp=other_core)
    cot_y.start()
    cot_core.start()
    cot_own = pltpu.make_async_copy(cot, cot_s.at[grp], clocal.at[0])
    cot_own.start()

    def ends(kind, at):
        cols = head_cols(head_at(at, idle))
        if kind == 0:
            return k.at[:, cols], k16.at[z + 4]
        if kind == 1:
            return v.at[:, cols], v16.at[z + 4]
        if kind == 2:
            return q.at[:, cols], q8.at[z]
        if kind == 3:
            return g_loc.at[head_at(at, idle)], g8.at[z]
        return nb_o, nb_v.at[z]

    def send(kind, at):
        src, dst = ends(kind, at)
        return remote(src, dst, ssem.at[kind, at], rsem.at[kind, z], tile=base + at)

    def keep(kind):
        src, dst = ends(kind, z)
        return pltpu.make_async_copy(src, dst, lsem.at[kind])

    def arrived(kind, at):
        dst = (k16.at[at + 4], v16.at[at + 4], q8.at[at], g8.at[at], nb_v.at[at])[kind]
        return remote(dst, dst, ssem.at[kind, 0], rsem.at[kind, at], tile=base + at)

    def send_kinds(kinds):
        @pl.loop(1, RING)
        def _(s):
            at = (z + s) % RING

            @pl.when(owns(at, idle))
            def _():
                for kind in kinds:
                    send(kind, at).start()

        @pl.when(mine)
        def _():
            for kind in kinds:
                keep(kind).start()

    down = lax.broadcasted_iota(jnp.int32, (8, 128), 0)
    across = lax.broadcasted_iota(jnp.int32, (8, 128), 1)
    table = jnp.zeros((8, 128), jnp.int32)
    ids = [listed[0, j] for j in range(NB)]
    for j, n in enumerate(ids):
        near = jnp.where(n >= 0, n - ring * RING + 4, z + 4)
        near = jnp.clip(near, 0, 2 * RING - 1)
        table = jnp.where((down == 0) & (across == j), near, table)
        alive = jnp.where(n >= 0, tokens[jnp.maximum(n, 0)], 0)
        table = jnp.where((down == 1) & (across == j), alive, table)
    for c, (dt, dh) in enumerate(SHIFTS):
        slot = jnp.int32(NB)
        for j in range(1, NB):
            hit = (ids[j] >= 0) & (ids[j] == tile + dt * 4 + dh)
            slot = slot - jnp.where(hit, NB - j, 0)
        table = jnp.where((down == 2) & (across == c), jnp.maximum(slot, 0), table)
    nb_o[...] = table

    send_kinds((4, 0))
    send_kinds((2,))

    remote(cot, cot_s.at[other_y], csend.at[0], crecv.at[0], grp=other_y).wait_recv()
    cot_on = remote(cot_s.at[other_y], cot_s.at[other_y], csend.at[2], crecv.at[2], grp=other_core)
    cot_on.start()
    far = (other_core + 2) % GRP
    remote(cot, cot_s.at[other_core], csend.at[1], crecv.at[1], grp=other_core).wait_recv()
    remote(cot, cot_s.at[far], csend.at[2], crecv.at[2], grp=other_core).wait_recv()
    cot_own.wait()

    @pl.loop(0, HEADS)
    def _(h):
        total = None
        for b in range(GRP):
            part = nt(cot_s[b], w[head_cols(h), b * DBLK:(b + 1) * DBLK])
            total = part if total is None else total + part
        g_loc[h] = total.astype(BF16)

    send_kinds((1,))
    send_kinds((3,))

    def hop(kind, at, start):
        buf = (k16, v16)[kind]

        def go(c):
            if start:
                c.start()
            else:
                c.wait_send()

        @pl.when((at >= 4) & has_up)
        def _():
            go(remote(buf.at[at + 4], buf.at[at - 4], khsend.at[kind, at], khrecv.at[kind, at],
                      tile=tile + RING))

        @pl.when((at < 4) & has_down)
        def _():
            go(remote(buf.at[at + 4], buf.at[at + 12], khsend.at[kind, at], khrecv.at[kind, at],
                      tile=tile - RING))

    def hops_arrived(kind):
        buf = (k16, v16)[kind]

        @pl.loop(0, RING)
        def _(at):
            @pl.when((at >= 4) & has_down)
            def _():
                remote(buf.at[at - 4], buf.at[at - 4], khsend.at[kind, at], khrecv.at[kind, at],
                       tile=tile - RING).wait_recv()

            @pl.when((at < 4) & has_up)
            def _():
                remote(buf.at[at + 12], buf.at[at + 12], khsend.at[kind, at], khrecv.at[kind, at],
                       tile=tile + RING).wait_recv()

    def back_ends(kind, at, h):
        src = (att8, dq8, dkb, dvb)[kind].at[at]
        dst = (att_s, dq, dk, dv)[kind].at[:, head_cols(h)]
        return src, dst

    def back(kind, at):
        src, dst = back_ends(kind, at, my_head)
        return remote(src, dst, osend.at[kind, at], orecv.at[kind, my_head], tile=base + at)

    def back_own(kind):
        src, dst = back_ends(kind, z, my_head)
        return pltpu.make_async_copy(src, dst, olocal.at[kind])

    def back_start(kind, at):
        @pl.when(at != z)
        def _():
            back(kind, at).start()

        @pl.when(at == z)
        def _():
            back_own(kind).start()

    def back_arrived(kind):
        @pl.loop(0, HEADS)
        def _(h):
            at = place_of(h, idle)
            src, dst = back_ends(kind, z, h)

            @pl.when(at != z)
            def _():
                remote(src, dst, osend.at[kind, 0], orecv.at[kind, h], tile=base + at).wait_recv()

        @pl.when(mine)
        def _():
            back_own(kind).wait()

    def local(r, j):
        return nb_s[r, 0, j]

    def count(r, j):
        return nb_s[r, 1, j]

    def gather(acc, r):
        acc[r + 5] += tmp[0]
        for n, (dt, dh) in enumerate(SHIFTS):
            acc[r + 5 + dt * 4 + dh] += tmp[nb_s[r, 2, n]]

    def weigh(r):
        queries = q8[r]
        rows = lax.broadcasted_iota(jnp.int32, (TILE, TILE), 0)
        top = jnp.full((8, TILE), -1e30, F32)
        for j in range(NB):
            s = nt(k16[local(r, j)], queries)
            s = jnp.where(rows < count(r, j), s, F32(-1e30))
            s_scr[j * TILE:(j + 1) * TILE, :] = s
            top = jnp.maximum(top, jnp.max(s.reshape(TILE // 8, 8, TILE), axis=0))
        top = jnp.max(top, axis=0, keepdims=True)
        total = jnp.zeros((8, TILE), F32)
        for j in range(NB):
            e = jnp.exp2((s_scr[j * TILE:(j + 1) * TILE, :] - top) * F32(FACTOR * LOG2E))
            s_scr[j * TILE:(j + 1) * TILE, :] = e
            total = total + jnp.sum(e.reshape(TILE // 8, 8, TILE), axis=0)
        inverse = 1.0 / jnp.sum(total, axis=0, keepdims=True)
        for j in range(NB):
            p[r, j * TILE:(j + 1) * TILE, :] = (
                s_scr[j * TILE:(j + 1) * TILE, :] * inverse
            ).astype(BF16)

    def attend(r):
        for j in range(NB):
            vc[j * TILE:(j + 1) * TILE, :] = v16[local(r, j)]
        out = tn(vc[...], p[r])
        o_t[r] = out
        att8[r] = out.T.astype(BF16)

    def value_part(r):
        tmp[0:NB] = jnp.dot(p[r], g8[r], preferred_element_type=F32).reshape(NB, TILE, HEAD_DIM)
        gather(accv, r)

    def score_part(r):
        grads = g8[r]
        delta = jnp.sum(o_t[r] * grads.astype(F32).T, axis=0, keepdims=True)
        for j in range(NB):
            rows = slice(j * TILE, (j + 1) * TILE)
            at = local(r, j)
            gp = nt(v16[at], grads)
            ds_s[rows, :] = (p[r, rows, :].astype(F32) * ((gp - delta) * F32(FACTOR))).astype(BF16)
            kc[rows, :] = k16[at]
        keys = jnp.dot(ds_s[...], q8[r], preferred_element_type=F32)
        tmp[0:NB] = keys.reshape(NB, TILE, HEAD_DIM)
        dq8[r] = tn(kc[...], ds_s[...]).T.astype(BF16)
        gather(acck, r)

    def halo(kind, up):
        src, dst = ((hks, hk), (hvs, hv))[kind]
        if up:
            return remote(src.at[pl.ds(4, 4)], dst.at[pl.ds(0, 4)], hsend.at[kind, 1],
                          hrecv.at[kind, 0], tile=tile + RING)
        return remote(src.at[pl.ds(0, 4)], dst.at[pl.ds(4, 4)], hsend.at[kind, 0],
                      hrecv.at[kind, 1], tile=tile - RING)

    def halo_start(kind):
        acc, src = ((acck, hks), (accv, hvs))[kind]

        @pl.when(has_down)
        def _():
            @pl.loop(0, 4)
            def _(i):
                src[i] = acc[i + 1].astype(BF16)
            halo(kind, False).start()

        @pl.when(has_up)
        def _():
            @pl.loop(0, 4)
            def _(i):
                src[i + 4] = acc[i + 13].astype(BF16)
            halo(kind, True).start()

    def home(kind):
        acc, got, out = ((acck, hk, dkb), (accv, hv, dvb))[kind]

        @pl.when(has_down)
        def _():
            halo(kind, True).wait_recv()

        @pl.when(has_up)
        def _():
            halo(kind, False).wait_recv()

        @pl.loop(0, RING)
        def _(s):
            at = (z + s) % RING
            given = ((at < 4) & has_down) | ((at >= 4) & has_up)

            @pl.when(given)
            def _():
                out[at] = (acc[at + 5] + got[at].astype(F32)).astype(BF16)

            @pl.when(jnp.logical_not(given))
            def _():
                out[at] = acc[at + 5].astype(BF16)

            back_start(2 + kind, at)

    def blk(i, size):
        return pl.ds(pl.multiple_of(i % 4 * size, size), size)

    class Line:
        def __init__(self, src, first, size, land, stage, slot):
            a, b = pl.ds(first, QUARTER), pl.ds(first + QUARTER, QUARTER)
            self.src, self.cols, self.size, self.land, self.stage = src, (a, b), size, land, stage

            def leg(i, col, n, to):
                return remote(src.at[blk(i, size), col], land.at[n], xsend.at[slot + n],
                              xrecv.at[slot + n], tile=to)

            self.rel = (leg(x + 2, a, 0, left), leg(x + 2, b, 1, right))
            self.one = (leg(x + 1, a, 2, right), leg(x + 3, b, 3, left))
            self.sum = tuple(
                remote(stage.at[n], land.at[4 + n], xsend.at[slot + 4 + n], xrecv.at[slot + 4 + n],
                       tile=(left, right)[n])
                for n in range(2)
            )

        def start(self):
            for c in self.rel + self.one:
                c.start()

        def relay(self):
            for n in range(2):
                self.rel[n].wait_recv()
                mine_too = self.src[blk(x + (3, 1)[n], self.size), self.cols[n]]
                self.stage[n] = (self.land[n].astype(F32) + mine_too.astype(F32)).astype(BF16)
                self.sum[n].start()

        def total(self, n):
            self.one[n].wait_recv()
            self.sum[n].wait_recv()
            here = self.src[blk(x, self.size), self.cols[n]]
            return here.astype(F32) + self.land[2 + n].astype(F32) + self.land[4 + n].astype(F32)

        def sent(self):
            for c in self.rel + self.one + self.sum:
                c.wait_send()

    first = Line(dwp, 0, XROWS, x1, xs1, 0)
    second = Line(y2, 0, SROWS, x2, xs2, 6)

    def half_rows(i):
        return pl.ds(pl.multiple_of(i * YROWS, YROWS), YROWS)

    y2_send = remote(dwp.at[half_rows(1 - y), pl.ds(HALF, HALF)], y2l, ysend.at[0], yrecv.at[0],
                     tile=y_pair)
    y1_send = remote(y1s, y1l, ysend.at[1], yrecv.at[1], tile=y_pair)
    to_core = remote(pos, pol, gsend.at[0], grecv.at[0], grp=other_core)
    to_y = remote(ybs, ybl, gsend.at[1], grecv.at[1], grp=other_y)

    def projected(b):
        cols = pl.ds(pl.multiple_of(b * DBLK, DBLK), DBLK)
        return jnp.dot(att_s[...], w[:, cols], preferred_element_type=F32)

    def stage_1():
        back_arrived(0)

        @pl.loop(0, HEADS)
        def _(h):
            rows = head_cols(h)
            turned = att_s[:, rows].T
            for b in range(GRP):
                dwp[rows, b * DBLK:(b + 1) * DBLK] = jnp.dot(
                    turned, cot_s[b], preferred_element_type=F32
                ).astype(BF16)

        y2_send.start()
        first.start()

        @pl.loop(0, 2)
        def _(yy):
            pos[yy] = projected(yy * 2 + 1 - core)

        to_core.start()

        @pl.loop(0, 2)
        def _(yy):
            own[yy] = projected(yy * 2 + core)

    def stage_2():
        first.relay()

    def stage_3():
        y2_send.wait_recv()
        y2[...] = (
            dwp[half_rows(y), HALF:].astype(F32) + y2l[...].astype(F32)
        ).astype(BF16)
        second.start()
        to_core.wait_recv()
        ybs[...] = (own[1 - y_hi] + pol[1 - y_hi]).astype(BF16)
        to_y.start()

    def mid_rows(i):
        return pl.ds(pl.multiple_of(i * SROWS, SROWS), SROWS)

    def stage_4():
        for n in range(2):
            cols = slice(n * QUARTER, (n + 1) * QUARTER)
            total = first.total(n)
            x_tot[n] = total
            y1s[:, cols] = x_tot[n, mid_rows(1 - y), :].astype(BF16)
        y1_send.start()
        second.relay()

    def stage_5():
        for n in range(2):
            zs[:, HALF + n * QUARTER:HALF + (n + 1) * QUARTER] = second.total(n).astype(BF16)
        y1_send.wait_recv()
        for n in range(2):
            cols = slice(n * QUARTER, (n + 1) * QUARTER)
            zs[:, cols] = (x_tot[n, mid_rows(y), :] + y1l[:, cols].astype(F32)).astype(BF16)

        @pl.loop(1, RING)
        def _(s):
            z_sum(s).start()

    def zpart(at):
        return (
            pl.ds(pl.multiple_of(at // 4 * ZROWS, ZROWS), ZROWS),
            pl.ds(pl.multiple_of(at % 4 * ZCOLS, ZCOLS), ZCOLS),
        )

    def z_sum(s):
        at = (z + s) % RING
        return remote(zs.at[zpart(at)], zl.at[z], zsend.at[0, s], zrecv.at[0, z], tile=base + at)

    def finished(at):
        row = jnp.where(at % 4 < 2, x * XROWS + y * SROWS, y * YROWS + x * SROWS)
        rows = pl.ds(pl.multiple_of(row + at // 4 * ZROWS, ZROWS), ZROWS)
        return dw.at[rows, zpart(at)[1]]

    def z_all(s):
        at = (z + s) % RING
        return remote(fin, finished(z), zsend.at[1, s], zrecv.at[1, z], tile=base + at)

    fin_own = pltpu.make_async_copy(fin, finished(z), olocal.at[4])

    def stage_6():
        rows, cols = zpart(z)
        total = zs[rows, cols].astype(F32)
        for s in range(1, RING):
            at = (z + s) % RING
            remote(zl.at[at], zl.at[at], zsend.at[0, 0], zrecv.at[0, at], tile=base + at).wait_recv()
            total += zl[at].astype(F32)
        fin[...] = total.astype(BF16)

        @pl.loop(1, RING)
        def _(s):
            z_all(s).start()

        fin_own.start()

    lo, hi = pl.ds(0, HALF), pl.ds(HALF, HALF)

    def slab_1y(yy):
        return dw.at[pl.ds(pl.multiple_of(x * XROWS + yy * SROWS, SROWS), SROWS), lo]

    def slab_2y(yy):
        return dw.at[half_rows(yy), hi]

    all_1y = remote(slab_1y(y), slab_1y(y), ysend.at[2], yrecv.at[2], tile=y_pair)
    got_1y = remote(slab_1y(1 - y), slab_1y(1 - y), ysend.at[2], yrecv.at[2], tile=y_pair)
    all_2y = remote(slab_2y(y), slab_2y(y), ysend.at[3], yrecv.at[3], tile=y_pair)
    got_2y = remote(slab_2y(1 - y), slab_2y(1 - y), ysend.at[3], yrecv.at[3], tile=y_pair)

    class Spread:
        def __init__(self, rows, cols, slot):
            def part(i, n, k, to):
                ref = dw.at[rows(i), pl.ds(cols + n * QUARTER, QUARTER)]
                return remote(ref, ref, xsend.at[slot + k], xrecv.at[slot + k], tile=to)

            self.outs = (
                part(x, 0, 0, right), part(x, 1, 1, left), part(x, 1, 2, right), part(x, 0, 3, left)
            )
            self.near = (part(x + 3, 0, 0, left), part(x + 1, 1, 1, right))
            self.on = (part(x + 3, 0, 4, right), part(x + 1, 1, 5, left))
            self.rest = (
                part(x + 3, 1, 2, left), part(x + 1, 0, 3, right),
                part(x + 2, 0, 4, left), part(x + 2, 1, 5, right),
            )

        def start(self):
            for c in self.outs:
                c.start()

        def relay(self):
            for n in range(2):
                self.near[n].wait_recv()
                self.on[n].start()

        def finish(self):
            for c in self.rest:
                c.wait_recv()

        def sent(self):
            for c in self.outs + self.on:
                c.wait_send()

    spread_1 = Spread(lambda i: blk(i, XROWS), 0, 12)
    spread_2 = Spread(
        lambda i: pl.ds(pl.multiple_of(y * YROWS + i % 4 * SROWS, SROWS), SROWS), HALF, 18
    )

    def stage_7():
        @pl.loop(1, RING)
        def _(s):
            at = (z + s) % RING
            remote(fin, finished(at), zsend.at[1, 0], zrecv.at[1, at], tile=base + at).wait_recv()

        fin_own.wait()
        spread_2.start()
        all_1y.start()

    def stage_8():
        to_y.wait_recv()
        bo[...] = (own[y_hi] + pol[y_hi] + ybl[...].astype(F32)).astype(BF16)
        spread_2.relay()
        got_1y.wait_recv()
        spread_1.start()
        spread_2.finish()
        all_2y.start()
        spread_1.relay()
        got_2y.wait_recv()
        spread_1.finish()

    @pl.when(mine)
    def _():
        acck[...] = jnp.zeros_like(acck)
        accv[...] = jnp.zeros_like(accv)
        tmp[NB] = jnp.zeros((TILE, HEAD_DIM), F32)
        keep(0).wait()
        hop(0, z, True)

        @pl.loop(1, RING)
        def _(s):
            at = (z + RING - s) % RING
            arrived(0, at).wait_recv()
            hop(0, at, True)

        for kind in (2, 4):
            keep(kind).wait()

            @pl.loop(1, RING)
            def _(s):
                arrived(kind, (z + s) % RING).wait_recv()

        lists = pltpu.make_async_copy(nb_v, nb_s, lsem.at[5])
        lists.start()
        hops_arrived(0)
        lists.wait()

        @pl.loop(0, RING)
        def _(i):
            weigh((z + i) % RING)

            @pl.when(i == 0)
            def _():
                keep(1).wait()
                hop(1, z, True)

            @pl.when(i > 0)
            def _():
                at = (z + RING - i) % RING
                arrived(1, at).wait_recv()
                hop(1, at, True)

        hops_arrived(1)

        @pl.loop(0, RING)
        def _(i):
            r = (z + i) % RING
            attend(r)
            back_start(0, r)

        keep(3).wait()

        @pl.loop(1, RING)
        def _(s):
            arrived(3, (z + s) % RING).wait_recv()

        @pl.loop(0, RING)
        def _(i):
            value_part((z + i) % RING)

        halo_start(1)

    stage_1()

    @pl.loop(0, RING)
    def _(i):
        @pl.when(mine)
        def _():
            r = (z + i) % RING
            score_part(r)
            back_start(1, r)

            @pl.when(i == 2)
            def _():
                home(1)

        @pl.when(i == 3)
        def _():
            stage_2()

        @pl.when(i == 5)
        def _():
            stage_3()

    @pl.when(mine)
    def _():
        halo_start(0)

    stage_4()

    @pl.when(mine)
    def _():
        home(0)

    stage_5()
    stage_6()
    stage_7()
    stage_8()

    for kind in (1, 2, 3):
        back_arrived(kind)

    @pl.loop(1, RING)
    def _(s):
        at = (z + s) % RING

        @pl.when(owns(at, idle))
        def _():
            for kind in range(5):
                send(kind, at).wait_send()

        @pl.when(mine)
        def _():
            for kind in range(4):
                back(kind, at).wait_send()

        z_sum(s).wait_send()
        z_all(s).wait_send()

    @pl.when(mine)
    def _():
        @pl.loop(0, RING)
        def _(at):
            for kind in (0, 1):
                hop(kind, at, False)

        for kind in (0, 1):
            @pl.when(has_down)
            def _():
                halo(kind, False).wait_send()

            @pl.when(has_up)
            def _():
                halo(kind, True).wait_send()

    for c in (cot_y, cot_core, cot_on, y2_send, y1_send, to_core, to_y, all_1y, all_2y):
        c.wait_send()
    for c in (first, second, spread_1, spread_2):
        c.sent()


def step(listed, tokens, q, k, v, cot, w):
    any_space = pl.BlockSpec(memory_space=pl.ANY)
    vmem = pl.BlockSpec(memory_space=pltpu.VMEM)
    smem = pl.BlockSpec(memory_space=pltpu.SMEM)
    dma = pltpu.SemaphoreType.DMA
    grad = jax.ShapeDtypeStruct((TILE, FEAT), BF16)

    def tiles(n, dtype=BF16):
        return pltpu.VMEM((n, TILE, HEAD_DIM), dtype)

    return pl.pallas_call(
        step_kernel,
        out_shape=(
            jax.ShapeDtypeStruct((TILE, DBLK), BF16), grad, grad, grad,
            jax.ShapeDtypeStruct((FEAT, DOUT), BF16),
        ),
        in_specs=[smem, smem, any_space, any_space, any_space, vmem, vmem],
        out_specs=(vmem, any_space, any_space, any_space, any_space),
        scratch_shapes=[
            pltpu.VMEM((8, 128), jnp.int32),
            pltpu.VMEM((RING, 8, 128), jnp.int32),
            pltpu.SMEM((RING, 8, 128), jnp.int32),
            tiles(2 * RING),
            tiles(2 * RING),
            tiles(RING),
            tiles(RING),
            pltpu.VMEM((GRP, TILE, DBLK), BF16),
            tiles(HEADS),
            pltpu.VMEM((KEYS, TILE), F32),
            pltpu.VMEM((RING, KEYS, TILE), BF16),
            pltpu.VMEM((KEYS, HEAD_DIM), BF16),
            pltpu.VMEM((KEYS, HEAD_DIM), BF16),
            pltpu.VMEM((KEYS, TILE), BF16),
            tiles(NB + 1, F32),
            pltpu.VMEM((RING, HEAD_DIM, TILE), F32),
            tiles(2 * RING + 2, F32),
            tiles(2 * RING + 2, F32),
            tiles(RING),
            tiles(RING),
            pltpu.VMEM((TILE, FEAT), BF16),
            tiles(RING),
            tiles(RING),
            tiles(RING),
            tiles(RING),
            tiles(RING),
            tiles(RING),
            pltpu.VMEM((FEAT, DOUT), BF16),
            pltpu.VMEM((6, XROWS, QUARTER), BF16),
            pltpu.VMEM((6, SROWS, QUARTER), BF16),
            pltpu.VMEM((2, XROWS, QUARTER), BF16),
            pltpu.VMEM((2, SROWS, QUARTER), BF16),
            pltpu.VMEM((2, XROWS, QUARTER), F32),
            pltpu.VMEM((SROWS, HALF), BF16),
            pltpu.VMEM((SROWS, HALF), BF16),
            pltpu.VMEM((YROWS, HALF), BF16),
            pltpu.VMEM((YROWS, HALF), BF16),
            pltpu.VMEM((SROWS, DOUT), BF16),
            pltpu.VMEM((RING, ZROWS, ZCOLS), BF16),
            pltpu.VMEM((ZROWS, ZCOLS), BF16),
            pltpu.VMEM((2, TILE, DBLK), F32),
            pltpu.VMEM((2, TILE, DBLK), F32),
            pltpu.VMEM((2, TILE, DBLK), F32),
            pltpu.VMEM((TILE, DBLK), BF16),
            pltpu.VMEM((TILE, DBLK), BF16),
            dma((5, RING)),
            dma((5, RING)),
            dma((6,)),
            dma((3,)),
            dma((3,)),
            dma((1,)),
            dma((2, RING)),
            dma((2, RING)),
            dma((4, RING)),
            dma((4, HEADS)),
            dma((5,)),
            dma((2, 2)),
            dma((2, 2)),
            dma((24,)),
            dma((24,)),
            dma((4,)),
            dma((4,)),
            dma((2, RING)),
            dma((2, RING)),
            dma((2,)),
            dma((2,)),
        ],
        compiler_params=pltpu.CompilerParams(
            collective_id=0, has_side_effects=True, vmem_limit_bytes=VMEM_LIMIT
        ),
        name="step",
    )(listed, tokens, q, k, v, cot, w)


def body(query_tokens, key_tokens, value_tokens, w_out, cotangent, neighbours, tile_tokens):
    return step(
        neighbours, tile_tokens, query_tokens, key_tokens, value_tokens, cotangent, w_out
    )


def solution(mesh):
    placed = (
        P("tile", "grp"),
        P("tile", "grp"),
        P("tile", "grp"),
        P("grp", None),
        P("tile", "grp"),
        P("tile", None),
        P(),
    )
    return jax.shard_map(
        body,
        mesh=mesh,
        in_specs=placed,
        out_specs=(
            P("tile", "grp"),
            P("tile", "grp"),
            P("tile", "grp"),
            P("tile", "grp"),
            P("grp", None),
        ),
        check_vma=False,
    )
```

time: 1170 us -> 206 us (0.18); the launches traced: 1150 us -> 204 us
  blocking collectives: 473 us -> 0 us
  waiting for transfers between devices: 374 us -> 0 us
  Pallas kernels: 0 us -> 195 us
  starting transfers between devices: 100 us -> 0 us
  matrix products: 82.9 us -> 0 us
  other arithmetic: 58.8 us -> 0 us
  local copies, waits for them, and re-layouts: 50.1 us -> 7.92 us
  between operations: 14.4 us -> 0.66 us
    psum x1 -> x0, blocking collectives: 473 us -> none  [body(): weight_grad = lax.psum(weight_part, 'tile').astype(jnp.bfloat16)]
    ppermute x16 -> x0, waiting for transfers between devices: 374 us -> none  [from_behind(): lax.ppermute(value, axis, [(source, source + steps) for source in range(i...]
    pallas_call x0 -> x1, Pallas kernels: none -> 195 us  [step(): pl.pallas_call(step_kernel, out_shape=(jax.ShapeDtypeStruct((TILE, DBLK),...]
    ppermute x16 -> x0, starting transfers between devices: 99.9 us -> none  [from_behind(): lax.ppermute(value, axis, [(source, source + steps) for source in range(i...]
    dot_general x39 -> x0, matrix products: 82.9 us -> none  [the longest x6 16.8 us: head_pass(): lax.dot_general(weights, grad_rows, (((0,), (0,)), ((), ())), preferred_e...]
    scatter-add x2 -> x0, other arithmetic: 26.7 us -> none  [the longest x1 13.4 us: tile_step(): value_buffer.at[slot_index].add(dv_rows.reshape(-1, TILE, width_here))]
    convert_element_type x8 -> x0, other arithmetic: 13 us -> none  [the longest x1 6.05 us: body(): value_total.astype(jnp.bfloat16)]
  transfers between devices with their start and end apart: 18 -> 0, of which waited for: 6 -> 0; matrix products, arithmetic and copies ran while one was open for 4% -> 0% of each run, Pallas kernels for 0% -> 0%
where the time goes in v2:
time: 206 us; the launch traced here: 204 us
  Pallas kernels  195 us (95%)
  local copies, waits for them, and re-layouts  7.92 us (4%)
    pallas_call x1, Pallas kernels, step(): pl.pallas_call(step_kernel, out_shape=(jax.ShapeDtypeStruct((TILE, DBLK),...  195 us
    unnamed x9, local copies, waits for them, and re-layouts  7.92 us

profile of v2, /device:TPU:24, one launch (start us, length us, event | category | flops | bytes accessed | tf_op | source)
XLA Modules:
  0.0 203.5 jit_solution(3428840419388121351)
XLA Ops:
  0.6 195.0 %step.1 = (bf16[384,384]{1,0:T(8,128)(2,1)}, bf16[384,768]{1,0:T(8,128)(2,1)}, bf16[384,768]{1,0:T(8,128)(2,1)}, bf16[384,768]{1,0:T(8,128)(2,1)}, bf16[768,1536]{1,0:T(8,128)(2,1)}) custom-call(s32[1,5]{1,0:T(1,128)} %listed.1, s32[64]{0:T(128)} %tokens.1, bf16[384,768]{1,0:T(8,128)(2,1)} %q.1, bf16[384,768]{1,0:T(8,128)(2,1)} %k.1, bf16[384,768]{1,0:T(8,128)(2,1)} %v.1, ...), custom_call_target="tpu_custom_call" | custom-call | tf_op jit(solution)/shard_map/step/pallas_call | solution.py:781
  195.6 0.0 copy-start.1
  195.6 0.0 copy-start
  195.6 1.9 copy.17
  197.5 1.9 copy.18
  199.4 1.9 copy.19
  201.3 0.0 copy-done.1
  201.3 0.8 copy.20
  202.1 0.0 copy-done
  202.1 1.4 copy.21
Async XLA Ops:
  195.6 5.7 %copy-start.1 = (bf16[384,768]{1,0:T(8,128)(2,1)S(1)}, bf16[384,768]{1,0:T(8,128)(2,1)}, u32[]{:S(2)}) copy-start(bf16[384,768]{1,0:T(8,128)(2,1)} %get-tuple-element.13) | copy-start | bytes 1769476
  195.6 6.5 %copy-start = (bf16[768,1536]{1,0:T(8,128)(2,1)S(1)}, bf16[768,1536]{1,0:T(8,128)(2,1)}, u32[]{:S(2)}) copy-start(bf16[768,1536]{1,0:T(8,128)(2,1)} %get-tuple-element.14) | copy-start | bytes 7077892

commit v3 on v2

--- a/solution.py
+++ b/solution.py
@@ -107,7 +107,7 @@
 def step_kernel(
     listed, tokens, q, k, v, cot, w,
     bo, dq, dk, dv, dw,
-    nb_o, nb_v, nb_s, k16, v16, q8, g8, cot_s, g_loc, s_scr, p, vc, kc, ds_s, tmp, o_t, acck, accv,
+    nb_o, nb_v, nb_s, k16, v16, q8, g8, cot_s, g_loc, s_scr, p, vc, tmp, o_t, acck, accv,
     att8, dq8, att_s, hk, hv, hks, hvs, dkb, dvb,
     dwp, x1, x2, xs1, xs2, x_tot, y1s, y1l, y2l, y2, zs, zl, fin, pos, pol, own, ybs, ybl,
     ssem, rsem, lsem, csend, crecv, clocal, khsend, khrecv, osend, orecv, olocal, hsend, hrecv,
@@ -335,19 +335,22 @@
         tmp[0:NB] = jnp.dot(p[r], g8[r], preferred_element_type=F32).reshape(NB, TILE, HEAD_DIM)
         gather(accv, r)
 
-    def score_part(r):
+    def key_part(r):
         grads = g8[r]
         delta = jnp.sum(o_t[r] * grads.astype(F32).T, axis=0, keepdims=True)
         for j in range(NB):
             rows = slice(j * TILE, (j + 1) * TILE)
-            at = local(r, j)
-            gp = nt(v16[at], grads)
-            ds_s[rows, :] = (p[r, rows, :].astype(F32) * ((gp - delta) * F32(FACTOR))).astype(BF16)
-            kc[rows, :] = k16[at]
-        keys = jnp.dot(ds_s[...], q8[r], preferred_element_type=F32)
+            gp = nt(v16[local(r, j)], grads)
+            ds = p[r, rows, :].astype(F32) * ((gp - delta) * F32(FACTOR))
+            p[r, rows, :] = ds.astype(BF16)
+        keys = jnp.dot(p[r], q8[r], preferred_element_type=F32)
         tmp[0:NB] = keys.reshape(NB, TILE, HEAD_DIM)
-        dq8[r] = tn(kc[...], ds_s[...]).T.astype(BF16)
         gather(acck, r)
+
+    def query_part(r):
+        for j in range(NB):
+            vc[j * TILE:(j + 1) * TILE, :] = k16[local(r, j)]
+        dq8[r] = tn(vc[...], p[r]).T.astype(BF16)
 
     def halo(kind, up):
         src, dst = ((hks, hk), (hvs, hv))[kind]
@@ -642,50 +645,50 @@
             arrived(0, at).wait_recv()
             hop(0, at, True)
 
-        for kind in (2, 4):
-            keep(kind).wait()
-
-            @pl.loop(1, RING)
-            def _(s):
-                arrived(kind, (z + s) % RING).wait_recv()
+        keep(4).wait()
+
+        @pl.loop(1, RING)
+        def _(s):
+            arrived(4, (z + RING - s) % RING).wait_recv()
 
         lists = pltpu.make_async_copy(nb_v, nb_s, lsem.at[5])
         lists.start()
         hops_arrived(0)
         lists.wait()
 
+        def ready(kind, i):
+            @pl.when(i == 0)
+            def _():
+                keep(kind).wait()
+
+            @pl.when(i > 0)
+            def _():
+                arrived(kind, (z + RING - i) % RING).wait_recv()
+
         @pl.loop(0, RING)
         def _(i):
-            weigh((z + i) % RING)
-
-            @pl.when(i == 0)
-            def _():
-                keep(1).wait()
-                hop(1, z, True)
-
-            @pl.when(i > 0)
-            def _():
-                at = (z + RING - i) % RING
-                arrived(1, at).wait_recv()
-                hop(1, at, True)
+            ready(2, i)
+            weigh((z + RING - i) % RING)
+
+            @pl.when(i >= 4)
+            def _():
+                for n in range(2):
+                    s = (i - 4) * 2 + n
+                    ready(1, s)
+                    hop(1, (z + RING - s) % RING, True)
 
         hops_arrived(1)
 
         @pl.loop(0, RING)
         def _(i):
-            r = (z + i) % RING
+            r = (z + RING - i) % RING
             attend(r)
             back_start(0, r)
 
-        keep(3).wait()
-
-        @pl.loop(1, RING)
-        def _(s):
-            arrived(3, (z + s) % RING).wait_recv()
-
         @pl.loop(0, RING)
         def _(i):
-            value_part((z + i) % RING)
+            ready(3, i)
+            value_part((z + RING - i) % RING)
 
         halo_start(1)
 
@@ -695,35 +698,36 @@
     def _(i):
         @pl.when(mine)
         def _():
-            r = (z + i) % RING
-            score_part(r)
-            back_start(1, r)
-
-            @pl.when(i == 2)
+            key_part((z + i) % RING)
+
+            @pl.when(i == 3)
             def _():
                 home(1)
 
-        @pl.when(i == 3)
-        def _():
-            stage_2()
-
-        @pl.when(i == 5)
-        def _():
-            stage_3()
+        for n, stage in ((2, stage_2), (4, stage_3), (6, stage_4)):
+            pl.when(i == n)(stage)
 
     @pl.when(mine)
     def _():
         halo_start(0)
 
-    stage_4()
-
-    @pl.when(mine)
-    def _():
-        home(0)
-
     stage_5()
-    stage_6()
-    stage_7()
+
+    @pl.loop(0, RING)
+    def _(i):
+        @pl.when(mine)
+        def _():
+            r = (z + i) % RING
+            query_part(r)
+            back_start(1, r)
+
+            @pl.when(i == 5)
+            def _():
+                home(0)
+
+        for n, stage in ((4, stage_6), (7, stage_7)):
+            pl.when(i == n)(stage)
+
     stage_8()
 
     for kind in (1, 2, 3):
@@ -799,8 +803,6 @@
             pltpu.VMEM((KEYS, TILE), F32),
             pltpu.VMEM((RING, KEYS, TILE), BF16),
             pltpu.VMEM((KEYS, HEAD_DIM), BF16),
-            pltpu.VMEM((KEYS, HEAD_DIM), BF16),
-            pltpu.VMEM((KEYS, TILE), BF16),
             tiles(NB + 1, F32),
             pltpu.VMEM((RING, HEAD_DIM, TILE), F32),
             tiles(2 * RING + 2, F32),
@@ -861,9 +863,37 @@
     )(listed, tokens, q, k, v, cot, w)
 
 
+def settle_kernel(*refs):
+    count = len(refs) // 2
+    sems = refs[-1]
+    copies = []
+    for n in range(count):
+        src, dst = refs[n], refs[count + n]
+        rows = src.shape[0] // 4
+        for part in range(4):
+            here = pl.ds(part * rows, rows)
+            copies.append(pltpu.make_async_copy(src.at[here], dst.at[here], sems.at[n, part]))
+    for c in copies:
+        c.start()
+    for c in copies:
+        c.wait()
+
+
+def settle(arrays):
+    any_space = pl.BlockSpec(memory_space=pl.ANY)
+    return pl.pallas_call(
+        settle_kernel,
+        out_shape=tuple(jax.ShapeDtypeStruct(a.shape, a.dtype) for a in arrays),
+        in_specs=[any_space] * len(arrays),
+        out_specs=(any_space,) * len(arrays),
+        scratch_shapes=[pltpu.SemaphoreType.DMA((len(arrays), 4))],
+        name="settle",
+    )(*arrays)
+
+
 def body(query_tokens, key_tokens, value_tokens, w_out, cotangent, neighbours, tile_tokens):
-    return step(
-        neighbours, tile_tokens, query_tokens, key_tokens, value_tokens, cotangent, w_out
+    return settle(
+        step(neighbours, tile_tokens, query_tokens, key_tokens, value_tokens, cotangent, w_out)
     )
 
 

time: 206 us -> 318 us (1.54)
  Pallas kernels: 195 us -> 314 us
  local copies, waits for them, and re-layouts: 7.92 us -> 0 us
    pallas_call x0 -> x1, Pallas kernels: none -> 135 us  [settle(): pl.pallas_call(settle_kernel, out_shape=tuple((jax.ShapeDtypeStruct(a.sha...]
    pallas_call x1, Pallas kernels: 195 us -> 179 us  [step(): pl.pallas_call(step_kernel, out_shape=(jax.ShapeDtypeStruct((TILE, DBLK),...]
    unnamed x9 -> x0, local copies, waits for them, and re-layouts: 7.92 us -> none
where the time goes in v3:
time: 318 us; the launch traced here: 315 us
  Pallas kernels  314 us (99%)
    pallas_call x1, Pallas kernels, step(): pl.pallas_call(step_kernel, out_shape=(jax.ShapeDtypeStruct((TILE, DBLK),...  179 us
    pallas_call x1, Pallas kernels, settle(): pl.pallas_call(settle_kernel, out_shape=tuple((jax.ShapeDtypeStruct(a.sha...  135 us

profile of v3, /device:TPU:24, one launch (start us, length us, event | category | flops | bytes accessed | tf_op | source)
XLA Modules:
  0.0 314.7 jit_solution(14604488828433670994)
XLA Ops:
  0.6 178.8 %step.1 = (bf16[384,384]{1,0:T(8,128)(2,1)}, bf16[384,768]{1,0:T(8,128)(2,1)}, bf16[384,768]{1,0:T(8,128)(2,1)}, bf16[384,768]{1,0:T(8,128)(2,1)}, bf16[768,1536]{1,0:T(8,128)(2,1)}) custom-call(s32[1,5]{1,0:T(1,128)} %listed.1, s32[64]{0:T(128)} %tokens.1, bf16[384,768]{1,0:T(8,128)(2,1)} %q.1, bf16[384,768]{1,0:T(8,128)(2,1)} %k.1, bf16[384,768]{1,0:T(8,128)(2,1)} %v.1, ...), custom_call_target="tpu_custom_call" | custom-call | tf_op jit(solution)/shard_map/step/pallas_call | solution.py:785
  179.4 135.3 %settle.1 = (bf16[384,384]{1,0:T(8,128)(2,1)}, bf16[384,768]{1,0:T(8,128)(2,1)}, bf16[384,768]{1,0:T(8,128)(2,1)}, bf16[384,768]{1,0:T(8,128)(2,1)}, bf16[768,1536]{1,0:T(8,128)(2,1)}) custom-call(bf16[384,384]{1,0:T(8,128)(2,1)} %get-tuple-element.10.refs_0_, bf16[384,768]{1,0:T(8,128)(2,1)} %get-tuple-element.11.refs_1_, ...), custom_call_target="tpu_custom_call" | custom-call | tf_op jit(solution)/shard_map/settle/pallas_call | solution.py:884

commit v4 on v3

--- a/solution.py
+++ b/solution.py
@@ -220,7 +220,6 @@
         g_loc[h] = total.astype(BF16)
 
     send_kinds((1,))
-    send_kinds((3,))
 
     def hop(kind, at, start):
         buf = (k16, v16)[kind]
@@ -463,17 +462,22 @@
     def stage_1():
         back_arrived(0)
 
-        @pl.loop(0, HEADS)
-        def _(h):
-            rows = head_cols(h)
-            turned = att_s[:, rows].T
-            for b in range(GRP):
-                dwp[rows, b * DBLK:(b + 1) * DBLK] = jnp.dot(
-                    turned, cot_s[b], preferred_element_type=F32
-                ).astype(BF16)
-
+        def part(first_head, count, blocks):
+            @pl.loop(first_head, first_head + count)
+            def _(h):
+                rows = head_cols(h)
+                turned = att_s[:, rows].T
+                for b in blocks:
+                    dwp[rows, b * DBLK:(b + 1) * DBLK] = jnp.dot(
+                        turned, cot_s[b], preferred_element_type=F32
+                    ).astype(BF16)
+
+        per_half = HEADS // 2
+        part((1 - y) * per_half, per_half, (2, 3))
         y2_send.start()
+        part(0, HEADS, (0, 1))
         first.start()
+        part(y * per_half, per_half, (2, 3))
 
         @pl.loop(0, 2)
         def _(yy):
@@ -620,14 +624,18 @@
         all_1y.start()
 
     def stage_8():
-        to_y.wait_recv()
-        bo[...] = (own[y_hi] + pol[y_hi] + ybl[...].astype(F32)).astype(BF16)
         spread_2.relay()
         got_1y.wait_recv()
         spread_1.start()
+        to_y.wait_recv()
+        bo[...] = (own[y_hi] + pol[y_hi] + ybl[...].astype(F32)).astype(BF16)
+
+    def stage_9():
         spread_2.finish()
         all_2y.start()
         spread_1.relay()
+
+    def stage_10():
         got_2y.wait_recv()
         spread_1.finish()
 
@@ -685,50 +693,58 @@
             attend(r)
             back_start(0, r)
 
+    @pl.when(jnp.logical_not(mine))
+    def _():
+        @pl.loop(1, RING)
+        def _(s):
+            at = (z + s) % RING
+
+            @pl.when(owns(at, idle))
+            def _():
+                send(1, at).wait_send()
+
+    send_kinds((3,))
+    stage_1()
+
+    def steps(work, stages):
         @pl.loop(0, RING)
         def _(i):
-            ready(3, i)
-            value_part((z + RING - i) % RING)
-
-        halo_start(1)
-
-    stage_1()
-
-    @pl.loop(0, RING)
-    def _(i):
-        @pl.when(mine)
-        def _():
-            key_part((z + i) % RING)
-
-            @pl.when(i == 3)
-            def _():
-                home(1)
-
-        for n, stage in ((2, stage_2), (4, stage_3), (6, stage_4)):
-            pl.when(i == n)(stage)
-
-    @pl.when(mine)
-    def _():
-        halo_start(0)
-
-    stage_5()
-
-    @pl.loop(0, RING)
-    def _(i):
-        @pl.when(mine)
-        def _():
-            r = (z + i) % RING
-            query_part(r)
-            back_start(1, r)
-
-            @pl.when(i == 5)
-            def _():
-                home(0)
-
-        for n, stage in ((4, stage_6), (7, stage_7)):
-            pl.when(i == n)(stage)
-
-    stage_8()
+            pl.when(mine)(lambda: work(i))
+            for n, stage in stages:
+                pl.when(i == n)(stage)
+
+    def owner(stage):
+        return lambda: pl.when(mine)(stage)
+
+    def value_step(i):
+        @pl.when(i == 0)
+        def _():
+            keep(3).wait()
+
+        @pl.when(i > 0)
+        def _():
+            arrived(3, (z + RING - i) % RING).wait_recv()
+
+        value_part((z + RING - i) % RING)
+
+    def query_step(i):
+        r = (z + i) % RING
+        query_part(r)
+        back_start(1, r)
+
+    steps(value_step, ((5, stage_2), (7, owner(lambda: halo_start(1)))))
+    steps(
+        lambda i: key_part((z + i) % RING),
+        (
+            (1, stage_3), (3, stage_4), (4, stage_5), (4, owner(lambda: home(1))), (6, stage_6),
+            (7, owner(lambda: halo_start(0))),
+        ),
+    )
+    steps(
+        query_step,
+        ((1, stage_7), (3, stage_8), (4, owner(lambda: home(0))), (6, stage_9)),
+    )
+    stage_10()
 
     for kind in (1, 2, 3):
         back_arrived(kind)
@@ -739,8 +755,12 @@
 
         @pl.when(owns(at, idle))
         def _():
-            for kind in range(5):
+            for kind in (0, 2, 3, 4):
                 send(kind, at).wait_send()
+
+            @pl.when(mine)
+            def _():
+                send(1, at).wait_send()
 
         @pl.when(mine)
         def _():
@@ -864,19 +884,25 @@
 
 
 def settle_kernel(*refs):
-    count = len(refs) // 2
+    count = (len(refs) - 1) // 3
     sems = refs[-1]
-    copies = []
-    for n in range(count):
-        src, dst = refs[n], refs[count + n]
+
+    def moves(n, part, leg):
+        src, dst, held = refs[n], refs[count + n], refs[2 * count + n]
         rows = src.shape[0] // 4
-        for part in range(4):
-            here = pl.ds(part * rows, rows)
-            copies.append(pltpu.make_async_copy(src.at[here], dst.at[here], sems.at[n, part]))
-    for c in copies:
-        c.start()
-    for c in copies:
-        c.wait()
+        here = pl.ds(part * rows, rows)
+        if leg == 0:
+            return pltpu.make_async_copy(src.at[here], held.at[here], sems.at[0, n, part])
+        return pltpu.make_async_copy(held.at[here], dst.at[here], sems.at[1, n, part])
+
+    every = [(n, part) for n in range(count) for part in range(4)]
+    for n, part in every:
+        moves(n, part, 0).start()
+    for n, part in every:
+        moves(n, part, 0).wait()
+        moves(n, part, 1).start()
+    for n, part in every:
+        moves(n, part, 1).wait()
 
 
 def settle(arrays):
@@ -886,7 +912,9 @@
         out_shape=tuple(jax.ShapeDtypeStruct(a.shape, a.dtype) for a in arrays),
         in_specs=[any_space] * len(arrays),
         out_specs=(any_space,) * len(arrays),
-        scratch_shapes=[pltpu.SemaphoreType.DMA((len(arrays), 4))],
+        scratch_shapes=[pltpu.VMEM(a.shape, a.dtype) for a in arrays]
+        + [pltpu.SemaphoreType.DMA((2, len(arrays), 4))],
+        compiler_params=pltpu.CompilerParams(vmem_limit_bytes=VMEM_LIMIT),
         name="settle",
     )(*arrays)
 

time: 318 us -> 186 us (0.58)
  Pallas kernels: 314 us -> 184 us
    pallas_call x1, Pallas kernels: 135 us -> 4.47 us  [settle(): pl.pallas_call(settle_kernel, out_shape=tuple((jax.ShapeDtypeStruct(a.sha...]
where the time goes in v4:
time: 186 us; the launch traced here: 184 us
  Pallas kernels  184 us (99%)
    pallas_call x1, Pallas kernels, step(): pl.pallas_call(step_kernel, out_shape=(jax.ShapeDtypeStruct((TILE, DBLK),...  179 us
    pallas_call x1, Pallas kernels, settle(): pl.pallas_call(settle_kernel, out_shape=tuple((jax.ShapeDtypeStruct(a.sha...  4.47 us

profile of v4, /device:TPU:24, one launch (start us, length us, event | category | flops | bytes accessed | tf_op | source)
XLA Modules:
  0.0 184.3 jit_solution(11296934940874636435)
XLA Ops:
  0.6 179.1 %step.1 = (bf16[384,384]{1,0:T(8,128)(2,1)}, bf16[384,768]{1,0:T(8,128)(2,1)}, bf16[384,768]{1,0:T(8,128)(2,1)}, bf16[384,768]{1,0:T(8,128)(2,1)}, bf16[768,1536]{1,0:T(8,128)(2,1)}) custom-call(s32[1,5]{1,0:T(1,128)} %listed.1, s32[64]{0:T(128)} %tokens.1, bf16[384,768]{1,0:T(8,128)(2,1)} %q.1, bf16[384,768]{1,0:T(8,128)(2,1)} %k.1, bf16[384,768]{1,0:T(8,128)(2,1)} %v.1, ...), custom_call_target="tpu_custom_call" | custom-call | tf_op jit(solution)/shard_map/step/pallas_call | solution.py:805
  179.8 4.5 %settle.1 = (bf16[384,384]{1,0:T(8,128)(2,1)}, bf16[384,768]{1,0:T(8,128)(2,1)}, bf16[384,768]{1,0:T(8,128)(2,1)}, bf16[384,768]{1,0:T(8,128)(2,1)}, bf16[768,1536]{1,0:T(8,128)(2,1)}) custom-call(bf16[384,384]{1,0:T(8,128)(2,1)} %get-tuple-element.10.refs_0_, bf16[384,768]{1,0:T(8,128)(2,1)} %get-tuple-element.11.refs_1_, ...), custom_call_target="tpu_custom_call" | custom-call | tf_op jit(solution)/shard_map/settle/pallas_call | solution.py:910

commit v5 on v4

--- a/solution.py
+++ b/solution.py
@@ -359,38 +359,30 @@
         return remote(src.at[pl.ds(0, 4)], dst.at[pl.ds(4, 4)], hsend.at[kind, 0],
                       hrecv.at[kind, 1], tile=tile - RING)
 
-    def halo_start(kind):
+    def halo_start(kind, up):
         acc, src = ((acck, hks), (accv, hvs))[kind]
 
-        @pl.when(has_down)
+        @pl.when(has_up if up else has_down)
         def _():
             @pl.loop(0, 4)
             def _(i):
-                src[i] = acc[i + 1].astype(BF16)
-            halo(kind, False).start()
-
-        @pl.when(has_up)
-        def _():
-            @pl.loop(0, 4)
-            def _(i):
-                src[i + 4] = acc[i + 13].astype(BF16)
-            halo(kind, True).start()
-
-    def home(kind):
+                if up:
+                    src[i + 4] = acc[i + 13].astype(BF16)
+                else:
+                    src[i] = acc[i + 1].astype(BF16)
+            halo(kind, up).start()
+
+    def home(kind, later):
         acc, got, out = ((acck, hk, dkb), (accv, hv, dvb))[kind]
-
-        @pl.when(has_down)
-        def _():
-            halo(kind, True).wait_recv()
-
-        @pl.when(has_up)
-        def _():
-            halo(kind, False).wait_recv()
-
-        @pl.loop(0, RING)
+        given = has_up if later else has_down
+
+        @pl.when(given)
+        def _():
+            halo(kind, not later).wait_recv()
+
+        @pl.loop(0, 4)
         def _(s):
-            at = (z + s) % RING
-            given = ((at < 4) & has_down) | ((at >= 4) & has_up)
+            at = (z + s) % 4 + (4 if later else 0)
 
             @pl.when(given)
             def _():
@@ -714,7 +706,12 @@
                 pl.when(i == n)(stage)
 
     def owner(stage):
-        return lambda: pl.when(mine)(stage)
+        def run():
+            @pl.when(mine)
+            def _():
+                stage()
+
+        return run
 
     def value_step(i):
         @pl.when(i == 0)
@@ -732,17 +729,18 @@
         query_part(r)
         back_start(1, r)
 
-    steps(value_step, ((5, stage_2), (7, owner(lambda: halo_start(1)))))
+    steps(value_step, ((5, stage_2), (7, owner(lambda: (halo_start(1, False), halo_start(1, True))))))
     steps(
-        lambda i: key_part((z + i) % RING),
+        key_part,
         (
-            (1, stage_3), (3, stage_4), (4, stage_5), (4, owner(lambda: home(1))), (6, stage_6),
-            (7, owner(lambda: halo_start(0))),
+            (1, stage_3), (3, stage_4), (4, stage_5), (4, owner(lambda: (home(1, True), home(1, False)))),
+            (4, owner(lambda: halo_start(0, False))), (6, stage_6),
+            (7, owner(lambda: halo_start(0, True))), (7, owner(lambda: home(0, True))),
         ),
     )
     steps(
         query_step,
-        ((1, stage_7), (3, stage_8), (4, owner(lambda: home(0))), (6, stage_9)),
+        ((1, stage_7), (2, owner(lambda: home(0, False))), (3, stage_8), (6, stage_9)),
     )
     stage_10()
 

time: 186 us -> 185 us (level)
  no operation moved by 1% of the time
where the time goes in v5:
time: 185 us; the launch traced here: 184 us
  Pallas kernels  184 us (99%)
    pallas_call x1, Pallas kernels, step(): pl.pallas_call(step_kernel, out_shape=(jax.ShapeDtypeStruct((TILE, DBLK),...  179 us
    pallas_call x1, Pallas kernels, settle(): pl.pallas_call(settle_kernel, out_shape=tuple((jax.ShapeDtypeStruct(a.sha...  4.47 us

profile of v5, /device:TPU:24, one launch (start us, length us, event | category | flops | bytes accessed | tf_op | source)
XLA Modules:
  0.0 184.4 jit_solution(18222003888020733993)
XLA Ops:
  0.6 179.3 %step.1 = (bf16[384,384]{1,0:T(8,128)(2,1)}, bf16[384,768]{1,0:T(8,128)(2,1)}, bf16[384,768]{1,0:T(8,128)(2,1)}, bf16[384,768]{1,0:T(8,128)(2,1)}, bf16[768,1536]{1,0:T(8,128)(2,1)}) custom-call(s32[1,5]{1,0:T(1,128)} %listed.1, s32[64]{0:T(128)} %tokens.1, bf16[384,768]{1,0:T(8,128)(2,1)} %q.1, bf16[384,768]{1,0:T(8,128)(2,1)} %k.1, bf16[384,768]{1,0:T(8,128)(2,1)} %v.1, ...), custom_call_target="tpu_custom_call" | custom-call | tf_op jit(solution)/shard_map/step/pallas_call | solution.py:803
  180.0 4.5 %settle.1 = (bf16[384,384]{1,0:T(8,128)(2,1)}, bf16[384,768]{1,0:T(8,128)(2,1)}, bf16[384,768]{1,0:T(8,128)(2,1)}, bf16[384,768]{1,0:T(8,128)(2,1)}, bf16[768,1536]{1,0:T(8,128)(2,1)}) custom-call(bf16[384,384]{1,0:T(8,128)(2,1)} %get-tuple-element.10.refs_0_, bf16[384,768]{1,0:T(8,128)(2,1)} %get-tuple-element.11.refs_1_, ...), custom_call_target="tpu_custom_call" | custom-call | tf_op jit(solution)/shard_map/settle/pallas_call | solution.py:908
